TPU v7x, 128 devices: a whole 4x4x4 slice. The times are simulated.
128 devices in a mesh: tm: 8 (over x, core), space: 16 (over y, z).
Axes of the slice: x: 4, y: 4, z: 4, core: 2. Of those that a mesh axis runs over, the one named last changes fastest.
Arguments:
- frames: bfloat16 [16, 768, 48, 384], P('tm', 'space'), may hold values from -6 to 6
- peak_voxels: int32 [4, 3, 8, 240], P(None, None, 'tm', 'space'), may hold values from -15 to 15
- owners: int32 [7680, 1], P(('tm', 'space')), may hold values from 0 to 127; in each aligned block of 60 rows (0 to 59, 60 to 119, ...) at most 3 rows name the same one
- tile_cells: int32 [7680], P(('tm', 'space')), may hold values from 0 to 127
Outputs:
- velocity: float32 [4, 3, 8, 240], P(None, None, 'tm', 'space')
- tile_velocity: float32 [3, 16384], P(None, ('tm', 'space'))
Inputs may be any that keep to these rules, and one draw needn't show every extreme that they name: `owners`: in each aligned block of 60 rows (the rows of one device) at most 3 rows name the same owner; some owner is named by exactly 3 rows of a block.
All inputs are finite; a program needn't handle non-finite values.
Results may differ from a plain program's by a relative error of at most 0.0003.
Values may be sent and summed in bfloat16 or wider, within the bound.
A program may use at most 320 MiB of HBM per device.

v0:
```python
import jax
import jax.numpy as jnp
from jax import lax
from jax.sharding import PartitionSpec as P

W = 48
H = 16
WY = 1
WZ = 15
GAPS = 4
TCELLS = 128
S = 24


def extended(array, sides, width):
    for axis, dim in sides:
        count, length = (lax.axis_size(axis), array.shape[dim])
        up = [(i, (i + 1) % count) for i in range(count - 1)]
        down = [(j, i) for i, j in up]
        last = lax.slice_in_dim(array, length - width, length, axis=dim)
        leading = lax.slice_in_dim(array, 0, width, axis=dim)
        before = lax.ppermute(last, axis, up)
        after = lax.ppermute(leading, axis, down)
        array = jnp.concatenate([before, array, after], axis=dim)
    return array


def partner(array, axis, stride):
    return lax.ppermute(array, axis, [(i, i ^ 1 << stride) for i in range(lax.axis_size(axis))])


def unit_shift(axis_index, sign_value):
    return tuple((sign_value if position == axis_index else 0 for position in range(3)))


def window_fits(slab_first, slab_second, peak_block, gap_size):
    window_index = jnp.arange(WY * WZ, dtype=jnp.int32)
    y_anchor = S * (window_index // WZ)
    z_anchor = S * (window_index % WZ)
    weight_norm = float(W) ** (-1.5)

    def single_window(y_start, z_start, x_peak, y_peak, z_peak):
        zero_index = jnp.zeros((), jnp.int32)
        block_first = lax.dynamic_slice(slab_first, (zero_index, y_start, z_start), (W, W, W))
        block_second = lax.dynamic_slice(
            slab_second,
            (H - 1 + x_peak, H - 1 + y_start + y_peak, H - 1 + z_start + z_peak),
            (W + 2, W + 2, W + 2),
        )

        def shifted(offsets):
            piece = block_second[
                1 + offsets[0] : 1 + offsets[0] + W,
                1 + offsets[1] : 1 + offsets[1] + W,
                1 + offsets[2] : 1 + offsets[2] + W,
            ]
            return (
                jnp.einsum("xyz,xyz->", block_first, piece, preferred_element_type=jnp.float32)
                * weight_norm
            )

        centre = shifted((0, 0, 0))
        result_list = []
        for axis_index in range(3):
            lower_value = shifted(unit_shift(axis_index, -1))
            upper_value = shifted(unit_shift(axis_index, 1))
            curvature = jnp.maximum(2.0 * centre - upper_value - lower_value, 1.0)
            result_list.append(0.5 * (upper_value - lower_value) / curvature)
        return jnp.stack(result_list)

    fits = jax.vmap(single_window)(y_anchor, z_anchor, peak_block[0], peak_block[1], peak_block[2])
    return (peak_block.astype(jnp.float32) + fits.T) / gap_size


def pair_fits(first_set, second_set, peak_set, gap_size):

    def fit_slot(slab_first, slab_second, peak_block):
        return window_fits(slab_first, slab_second, peak_block, gap_size)

    return jax.vmap(fit_slot, in_axes=(0, 0, 1), out_axes=1)(first_set, second_set, peak_set)


def widen(frame_set):
    depth = frame_set.shape[3]
    spare = -(depth + 2 * H) % 128
    return jnp.pad(frame_set, ((0, 0), (0, 0), (H, H), (H, H + spare)))


def on_device(frames, peak_voxels, owners, tile_cells):
    per_device = frames.shape[0]
    half_count = per_device // 2
    local_bits = per_device.bit_length() - 1
    own_wide = extended(frames[1:], (("space", 1),), H)
    rim_base = 1
    gap_results = []
    for gap_index in range(GAPS):
        gap_size = 2**gap_index
        if gap_size < per_device:
            chosen = [0 // gap_size * 2 * gap_size + 0 % gap_size]
            first_set = jnp.stack([frames[frame_index] for frame_index in chosen])
            second_set = jnp.stack(
                [own_wide[frame_index + gap_size - rim_base] for frame_index in chosen]
            )
        else:
            tm_bit = gap_index - local_bits
            is_lower = lax.axis_index("tm") // 2**tm_bit % 2 == 0
            incoming = partner(frames, "tm", tm_bit)
            incoming = extended(incoming, (("space", 1),), H)
            partner_wide = jnp.where(is_lower, incoming[:half_count], incoming[half_count:])
            first_set = jnp.where(is_lower, frames[:half_count], partner_wide[:, H : H + W])
            second_set = jnp.where(is_lower, partner_wide, own_wide)
        gap_results.append(
            pair_fits(first_set, widen(second_set), peak_voxels[gap_index], gap_size)
        )
    velocity = jnp.stack(gap_results)
    listed = jnp.transpose(velocity, (1, 0, 2, 3)).reshape(3, -1)
    target = owners[:, 0]
    tm_count = lax.axis_size("tm")
    space_count = lax.axis_size("space")
    devices = tm_count * space_count
    capacity = 3 * target.shape[0] // devices + 2
    hits = (target[:, None] == jnp.arange(devices, dtype=jnp.int32)[None, :]).astype(jnp.int32)
    earlier = jnp.cumsum(hits, axis=0) - hits
    ranking = jnp.sum(earlier * hits, axis=1)
    slot_index = target * capacity + ranking
    send_velocity = jnp.zeros((3, devices * capacity), jnp.float32).at[:, slot_index].set(listed)
    send_cells = jnp.full((devices * capacity,), -1, jnp.int32).at[slot_index].set(tile_cells)
    arrived_velocity, arrived_cells = (
        lax.all_to_all(
            send_velocity.reshape(3, devices, capacity),
            ("tm", "space"),
            split_axis=1,
            concat_axis=1,
            tiled=True,
        ),
        lax.all_to_all(
            send_cells.reshape(1, devices, capacity),
            ("tm", "space"),
            split_axis=1,
            concat_axis=1,
            tiled=True,
        ),
    )
    arrived_velocity = arrived_velocity.reshape(3, -1)
    arrived_cells = arrived_cells.reshape(-1)
    matches = (arrived_cells[None, :] == jnp.arange(TCELLS, dtype=jnp.int32)[:, None]).astype(
        jnp.float32
    )
    cell_sums = jnp.einsum(
        "cs,ts->ct",
        arrived_velocity,
        matches,
        precision=lax.Precision.HIGHEST,
        preferred_element_type=jnp.float32,
    )
    counts = jnp.sum(matches, axis=1)
    tile_velocity = cell_sums / jnp.maximum(counts, 1.0)[None, :]
    return (velocity, tile_velocity)


def solution(mesh):
    placed = (
        P("tm", "space", None, None),
        P(None, None, "tm", "space"),
        P(("tm", "space"), None),
        P(("tm", "space")),
    )
    return jax.shard_map(
        on_device,
        mesh=mesh,
        in_specs=placed,
        out_specs=(P(None, None, "tm", "space"), P(None, ("tm", "space"))),
        check_vma=False,
    )
```

profile of v0, /device:TPU:1, one launch (start us, length us, event | category | flops | bytes accessed | tf_op | source)
XLA Modules:
  0.0 1047.1 jit_solution(13198463282662008032)
XLA Ops:
  8.8 4.2 collective-permute-start
  17.0 12.5 %all-to-all-start.1 = ((s32[1,128,3]{2,0,1:T(1,128)}), s32[1,128,3]{2,0,1:T(1,128)}, u32[]{:S(2)}, u32[]{:S(2)}) async-start(s32[1,128,3]{2,0,1:T(1,128)} %bitcast.82), calls=%async_computation.1 | async-start | bytes 131072 | tf_op jit(solution)/shard_map/all_to_all | solution.py:136
  32.3 3.6 fusion.51
  35.9 4.5 copy.208
  40.4 7.6 gather_fusion
  47.9 15.6 %copy.90 = f32[15,48,48,48]{3,2,1,0:T(8,128)} copy(bf16[15,48,48,48]{2,1,3,0:T(8,128)(2,1)} %gather_fusion) | data formatting | bytes 9953280
  63.5 101.4 %all-to-all-done.1 = s32[1,128,3]{2,0,1:T(1,128)} async-done(((s32[1,128,3]{2,0,1:T(1,128)}), s32[1,128,3]{2,0,1:T(1,128)}, u32[]{:S(2)}, u32[]{:S(2)}) %all-to-all-start.1) | async-done | bytes 1568 | tf_op jit(solution)/shard_map/all_to_all | solution.py:136
  170.9 5.1 pad.13
  176.1 5.5 broadcast.734.clone
  181.6 84.1 %while.4 = (s32[]{:T(128)}, bf16[1,80,80,512]{3,2,1,0:T(8,128)(2,1)}, s32[15,4]{0,1:T(4,128)S(1)}, bf16[15,50,50,50]{3,2,1,0:T(8,128)(2,1)}, s32[]{:T(128)}) while((s32[]{:T(128)}, bf16[1,80,80,512]{3,2,1,0:T(8,128)(2,1)}, s32[15,4]{0,1:T(4,128)S(1)}, bf16[15,50,50,50]{3,2,1,0:T(8,128)(2,1)}, s32[]{:T(128)}) %tuple.155), condition=%wide.while_cond, body=%wide.while_body.sunk | while | flops 2 | bytes 1435269 | solution.py:45
  182.2 4.9 dynamic-slice_dynamic-update-slice_fusion.2
  187.8 4.9 dynamic-slice_dynamic-update-slice_fusion.2
  193.4 4.9 dynamic-slice_dynamic-update-slice_fusion.2
  199.0 4.9 dynamic-slice_dynamic-update-slice_fusion.2
  204.6 4.9 dynamic-slice_dynamic-update-slice_fusion.2
  210.1 4.9 dynamic-slice_dynamic-update-slice_fusion.2
  215.7 5.0 dynamic-slice_dynamic-update-slice_fusion.2
  221.3 5.0 dynamic-slice_dynamic-update-slice_fusion.2
  226.9 5.0 dynamic-slice_dynamic-update-slice_fusion.2
  232.6 4.9 dynamic-slice_dynamic-update-slice_fusion.2
  238.1 5.0 dynamic-slice_dynamic-update-slice_fusion.2
  243.8 5.0 dynamic-slice_dynamic-update-slice_fusion.2
  249.5 4.9 dynamic-slice_dynamic-update-slice_fusion.2
  255.1 5.0 dynamic-slice_dynamic-update-slice_fusion.2
  260.7 5.0 dynamic-slice_dynamic-update-slice_fusion.2
  274.1 49.9 %multiply_reduce_fusion.27 = (f32[15]{0:T(128)}, f32[15]{0:T(128)}, f32[15]{0:T(128)}, f32[15]{0:T(128)}, f32[15]{0:T(128)}, /*index=5*/f32[15]{0:T(128)}, f32[15]{0:T(128)}) fusion(f32[15,48,48,48]{3,2,1,0:T(8,128)} %copy.90, bf16[1,15,50,50,50]{4,3,2,1,0:T(8,128)(2,1)} %bitcast.297), kind=kLoop, calls=%fused_computation.44 | loop fusion | flops 34836372 | bytes 29860260 | tf_op jit(solution)/shard_map/vmap(vmap(xyz,xyz->))/dot_general | solution.py:58
  324.1 13.9 %copy.68 = bf16[1,80,48,384]{2,1,3,0:T(8,128)(2,1)} copy(bf16[1,80,48,384]{3,2,1,0:T(8,128)(2,1)S(1)} %pad_maximum_fusion) | data formatting | bytes 5898240 | tf_op jit(solution)/shard_map/concatenate | solution.py:24
  340.9 4.0 collective-permute-start.9
  349.6 5.0 collective-permute-start.6
  363.8 5.0 collective-permute-done.9
  370.0 13.8 %copy.202 = bf16[1,80,48,384]{2,1,3,0:T(8,128)(2,1)} copy(bf16[1,80,48,384]{3,2,1,0:T(8,128)(2,1)} %get-tuple-element.181) | data formatting | bytes 5898240
  383.7 13.9 %copy.203 = bf16[1,80,48,384]{2,1,3,0:T(8,128)(2,1)} copy(bf16[1,80,48,384]{3,2,1,0:T(8,128)(2,1)S(1)} %get-tuple-element.180) | data formatting | bytes 5898240
  397.7 4.1 constant_dynamic-update-slice_fusion.10
  404.3 4.9 fusion.46
  409.2 13.8 %copy.206 = bf16[1,80,48,384]{2,1,3,0:T(8,128)(2,1)} copy(bf16[1,80,48,384]{3,2,1,0:T(8,128)(2,1)} %get-tuple-element.185) | data formatting | bytes 5898240
  423.0 13.9 %copy.207 = bf16[1,80,48,384]{2,1,3,0:T(8,128)(2,1)} copy(bf16[1,80,48,384]{3,2,1,0:T(8,128)(2,1)S(1)} %get-tuple-element.184) | data formatting | bytes 5898240
  444.7 13.8 %copy.204 = bf16[1,80,48,384]{2,1,3,0:T(8,128)(2,1)} copy(bf16[1,80,48,384]{3,2,1,0:T(8,128)(2,1)} %get-tuple-element.183) | data formatting | bytes 5898240
  458.5 13.9 %copy.205 = bf16[1,80,48,384]{2,1,3,0:T(8,128)(2,1)} copy(bf16[1,80,48,384]{3,2,1,0:T(8,128)(2,1)S(1)} %get-tuple-element.182) | data formatting | bytes 5898240
  472.5 27.7 %broadcast_select_fusion.4 = (bf16[1,80,48,384]{2,1,3,0:T(8,128)(2,1)}, bf16[1,80,48,384]{2,1,3,0:T(8,128)(2,1)}, bf16[1,80,48,384]{2,1,3,0:T(8,128)(2,1)}, bf16...) fusion(bf16[1,80,48,384]{2,1,3,0:T(8,128)(2,1)} %copy.68, ...), kind=kLoop, calls=%fused_computation.77 | loop fusion | flops 8847360 | bytes 38338564 | tf_op jit(solution)/shard_map/jit(_where)/select_n | solution.py:111
  500.2 12.3 %fusion.2 = (bf16[48,48,384]{1,0,2:T(8,128)(2,1)}, bf16[48,48,384]{1,0,2:T(8,128)(2,1)}, bf16[48,48,384]{1,0,2:T(8,128)(2,1)}) fusion(bf16[1,48,48,384]{2,1,3,0:T(8,128)(2,1)} %copy.208, bf16[1,80,48,384]{2,1,3,0:T(8,128)(2,1)} %get-tuple-element.159, pred[]{:T(512)S(6)} %eq.48, bf16[1,80,48,384]{2,1,3,0:T(8,128)(2,1)} %get-tuple-element.177, pred[]{:T(512)S(6)} %eq.50, ...), kind=kLoop, calls=%fused_computation.84 | loop fusion | flops 2654208 | bytes 12386307 | tf_op jit(solution)/shard_map/jit(_where)/select_n | solution.py:110
  512.5 7.6 gather_fusion.3
  520.1 15.6 %copy.174 = f32[15,48,48,48]{3,2,1,0:T(8,128)} copy(bf16[15,48,48,48]{2,1,3,0:T(8,128)(2,1)} %gather_fusion.3) | data formatting | bytes 9953280
  535.7 9.8 pad.16
  545.5 5.4 broadcast.734.clone.1
  550.9 84.3 %while.7 = (s32[]{:T(128)}, bf16[1,80,80,512]{2,1,3,0:T(8,128)(2,1)}, s32[15,4]{0,1:T(4,128)S(1)}, bf16[15,50,50,50]{3,2,1,0:T(8,128)(2,1)}, s32[]{:T(128)}) while((s32[]{:T(128)}, bf16[1,80,80,512]{2,1,3,0:T(8,128)(2,1)}, s32[15,4]{0,1:T(4,128)S(1)}, bf16[15,50,50,50]{3,2,1,0:T(8,128)(2,1)}, s32[]{:T(128)}) %tuple.169), condition=%wide.while_cond.3, body=%wide.while_body.3.sunk | while | flops 2 | bytes 1966945 | solution.py:45
  635.2 7.6 gather_fusion.2
  642.8 15.9 %copy.146 = f32[15,48,48,48]{3,2,1,0:T(8,128)} copy(bf16[15,48,48,48]{2,1,3,0:T(8,128)(2,1)} %gather_fusion.2) | data formatting | bytes 9953280
  658.7 9.7 pad.15
  668.4 5.5 broadcast.734.clone.2
  673.9 86.7 %while.6 = (s32[]{:T(128)}, bf16[1,80,80,512]{2,1,3,0:T(8,128)(2,1)}, s32[15,4]{0,1:T(4,128)S(1)}, bf16[15,50,50,50]{3,2,1,0:T(8,128)(2,1)}, s32[]{:T(128)}) while((s32[]{:T(128)}, bf16[1,80,80,512]{2,1,3,0:T(8,128)(2,1)}, s32[15,4]{0,1:T(4,128)S(1)}, bf16[15,50,50,50]{3,2,1,0:T(8,128)(2,1)}, s32[]{:T(128)}) %tuple.167), condition=%wide.while_cond.2, body=%wide.while_body.2.sunk | while | flops 2 | bytes 1966945 | solution.py:45
  674.6 3.6 constant_dynamic-slice_fusion.18
  686.1 3.6 constant_dynamic-slice_fusion.18
  697.7 3.6 constant_dynamic-slice_fusion.18
  703.5 3.6 constant_dynamic-slice_fusion.18
  760.6 7.5 gather_fusion.1
  768.2 15.6 %copy.118 = f32[15,48,48,48]{3,2,1,0:T(8,128)} copy(bf16[15,48,48,48]{2,1,3,0:T(8,128)(2,1)} %gather_fusion.1) | data formatting | bytes 9953280
  783.7 9.7 pad.14
  793.5 5.4 broadcast.734.clone.3
  798.8 83.5 %while.5 = (s32[]{:T(128)}, bf16[1,80,80,512]{2,1,3,0:T(8,128)(2,1)}, s32[15,4]{0,1:T(4,128)S(1)}, bf16[15,50,50,50]{3,2,1,0:T(8,128)(2,1)}, s32[]{:T(128)}) while((s32[]{:T(128)}, bf16[1,80,80,512]{2,1,3,0:T(8,128)(2,1)}, s32[15,4]{0,1:T(4,128)S(1)}, bf16[15,50,50,50]{3,2,1,0:T(8,128)(2,1)}, s32[]{:T(128)}) %tuple.168), condition=%wide.while_cond.1, body=%wide.while_body.1.sunk | while | flops 2 | bytes 1966945 | solution.py:45
  882.3 49.5 %multiply_reduce_fusion.6 = (f32[15]{0:T(128)S(1)}, f32[15]{0:T(128)S(1)}, f32[15]{0:T(128)S(1)}, f32[15]{0:T(128)S(1)}, f32[15]{0:T(128)S(1)}, /*index=5*/f32[15]{0:T(128)S(1)}, f32[15]{0:T(128)S(1)}) fusion(f32[15,48,48,48]{3,2,1,0:T(8,128)} %copy.174, bf16[1,15,50,50,50]{4,3,2,1,0:T(8,128)(2,1)} %bitcast.298), kind=kLoop, calls=%fused_computation.23 | loop fusion | flops 34836372 | bytes 29860260 | tf_op jit(solution)/shard_map/vmap(vmap(xyz,xyz->))/dot_general | solution.py:58
  931.8 49.7 %multiply_reduce_fusion.13 = (f32[15]{0:T(128)S(1)}, f32[15]{0:T(128)S(1)}, f32[15]{0:T(128)S(1)}, f32[15]{0:T(128)S(1)}, f32[15]{0:T(128)S(1)}, /*index=5*/f32[15]{0:T(128)S(1)}, f32[15]{0:T(128)S(1)}) fusion(f32[15,48,48,48]{3,2,1,0:T(8,128)} %copy.146, bf16[1,15,50,50,50]{4,3,2,1,0:T(8,128)(2,1)} %bitcast.299), kind=kLoop, calls=%fused_computation.30 | loop fusion | flops 34836372 | bytes 29860260 | tf_op jit(solution)/shard_map/vmap(vmap(xyz,xyz->))/dot_general | solution.py:58
  981.6 37.2 %multiply_reduce_fusion.20 = (f32[15]{0:T(128)S(1)}, f32[15]{0:T(128)S(1)}, f32[15]{0:T(128)S(1)}, f32[15]{0:T(128)S(1)}, f32[15]{0:T(128)S(1)}, /*index=5*/f32[15]{0:T(128)S(1)}, f32[15]{0:T(128)S(1)}) fusion(f32[15,48,48,48]{3,2,1,0:T(8,128)} %copy.118, bf16[1,15,50,50,50]{4,3,2,1,0:T(8,128)(2,1)S(1)} %bitcast.296), kind=kLoop, calls=%fused_computation.37 | loop fusion | flops 34836372 | bytes 29860260 | tf_op jit(solution)/shard_map/vmap(vmap(xyz,xyz->))/dot_general | solution.py:58
  1021.3 13.2 %all-to-all-start = ((f32[3,128,3]{2,0,1:T(4,128)}), f32[3,128,3]{2,0,1:T(4,128)S(1)}, u32[]{:S(2)}, u32[]{:S(2)}) async-start(f32[3,128,3]{2,0,1:T(4,128)} %copy.83), calls=%async_computation | async-start | bytes 524288 | tf_op jit(solution)/shard_map/all_to_all | solution.py:129
  1035.2 10.6 %all-to-all-done = f32[3,128,3]{2,0,1:T(4,128)S(1)} async-done(((f32[3,128,3]{2,0,1:T(4,128)}), f32[3,128,3]{2,0,1:T(4,128)S(1)}, u32[]{:S(2)}, u32[]{:S(2)}) %all-to-all-start) | async-done | bytes 4640 | tf_op jit(solution)/shard_map/all_to_all | solution.py:129
  (358 shorter events, 311.4 us)
Async XLA Ops:
  0.6 265.0 %collective-permute-start.2 = (bf16[2,48,48,384]{3,2,1,0:T(8,128)(2,1)}, bf16[2,48,48,384]{3,2,1,0:T(8,128)(2,1)}, u32[]{:S(2)}, u32[]{:S(2)}) collective-permute-start(bf16[2,48,48,384]{3,2,1,0:T(8,128)(2,1)} %param.4), channel_id=1, source_target_pairs={{0,16},{16,0},{32,48},{48,32},{64,80},{80,64},{96,112},{112,96},{1... | collective-permute-start | bytes 10616840 | tf_op jit(solution)/shard_map/ppermute | solution.py:29
  2.1 335.9 %collective-permute-start.8 = (bf16[2,48,48,384]{3,2,1,0:T(8,128)(2,1)}, bf16[2,48,48,384]{3,2,1,0:T(8,128)(2,1)}, u32[]{:S(2)}, u32[]{:S(2)}) collective-permute-start(bf16[2,48,48,384]{3,2,1,0:T(8,128)(2,1)} %param.4), channel_id=1, source_target_pairs={{0,64},{16,80},{32,96},{48,112},{64,0},{80,16},{96,32},{112,48},{1... | collective-permute-start | bytes 10616840 | tf_op jit(solution)/shard_map/ppermute | solution.py:29
  5.0 341.3 %collective-permute-start.5 = (bf16[2,48,48,384]{3,2,1,0:T(8,128)(2,1)}, bf16[2,48,48,384]{3,2,1,0:T(8,128)(2,1)}, u32[]{:S(2)}, u32[]{:S(2)}) collective-permute-start(bf16[2,48,48,384]{3,2,1,0:T(8,128)(2,1)} %param.4), channel_id=1, source_target_pairs={{0,32},{16,48},{32,0},{48,16},{64,96},{80,112},{96,64},{112,80},{1... | collective-permute-start | bytes 10616840 | tf_op jit(solution)/shard_map/ppermute | solution.py:29
  7.5 160.6 %collective-permute-start.1 = (bf16[1,16,48,384]{3,2,1,0:T(8,128)(2,1)}, bf16[1,16,48,384]{3,2,1,0:T(8,128)(2,1)S(1)}, u32[]{:S(2)}, u32[]{:S(2)}) collective-permute-start(bf16[1,16,48,384]{3,2,1,0:T(8,128)(2,1)} %get-tuple-element.196), channel_id=1, source_target_pairs={{1,0},{2,1},{3,2},{4,3},{5,4},{6,5},{7,6},{8,7},{9,8},{10,9},{11,1... | collective-permute-start | bytes 1769480 | tf_op jit(solution)/shard_map/ppermute | solution.py:23
  8.8 159.3 %collective-permute-start = (bf16[1,16,48,384]{3,2,1,0:T(8,128)(2,1)S(1)}, bf16[1,16,48,384]{3,2,1,0:T(8,128)(2,1)S(1)}, u32[]{:S(2)}, u32[]{:S(2)}) collective-permute-start(bf16[1,16,48,384]{3,2,1,0:T(8,128)(2,1)S(1)} %get-tuple-element.195), channel_id=1, source_target_pairs={{0,1},{1,2},{2,3},{3,4},{4,5},{5,6},{6,7},{7,8},{8,9},{9,10},{10,1... | collective-permute-start | bytes 1769480 | tf_op jit(solution)/shard_map/ppermute | solution.py:22
  15.3 15.7 %copy-start.15 = (s32[60]{0:T(128)}, s32[60]{0:T(128)S(1)}, u32[]{:S(2)}) copy-start(s32[60]{0:T(128)S(1)} %fusion.26) | copy-start | bytes 724
  17.0 147.9 %all-to-all-start.1 = ((s32[1,128,3]{2,0,1:T(1,128)}), s32[1,128,3]{2,0,1:T(1,128)}, u32[]{:S(2)}, u32[]{:S(2)}) async-start(s32[1,128,3]{2,0,1:T(1,128)} %bitcast.82), calls=%async_computation.1 | async-start | bytes 131072 | tf_op jit(solution)/shard_map/all_to_all | solution.py:136
  167.4 0.7 copy-start.5
  168.1 0.8 copy-start
  268.9 85.6 %collective-permute-start.3 = (bf16[2,16,48,384]{3,2,1,0:T(8,128)(2,1)}, bf16[2,16,48,384]{3,2,1,0:T(8,128)(2,1)}, u32[]{:S(2)}, u32[]{:S(2)}) collective-permute-start(bf16[2,16,48,384]{3,2,1,0:T(8,128)(2,1)} %get-tuple-element.190), channel_id=1, source_target_pairs={{0,1},{1,2},{2,3},{3,4},{4,5},{5,6},{6,7},{7,8},{8,9},{9,10},{10,1... | collective-permute-start | bytes 3538952 | tf_op jit(solution)/shard_map/ppermute | solution.py:22
  272.4 87.8 %collective-permute-start.4 = (bf16[2,16,48,384]{3,2,1,0:T(8,128)(2,1)}, bf16[2,16,48,384]{3,2,1,0:T(8,128)(2,1)}, u32[]{:S(2)}, u32[]{:S(2)}) collective-permute-start(bf16[2,16,48,384]{3,2,1,0:T(8,128)(2,1)} %get-tuple-element.189), channel_id=1, source_target_pairs={{1,0},{2,1},{3,2},{4,3},{5,4},{6,5},{7,6},{8,7},{9,8},{10,9},{11,1... | collective-permute-start | bytes 3538952 | tf_op jit(solution)/shard_map/ppermute | solution.py:23
  340.9 27.9 %collective-permute-start.9 = (bf16[2,16,48,384]{3,2,1,0:T(8,128)(2,1)S(1)}, bf16[2,16,48,384]{3,2,1,0:T(8,128)(2,1)S(1)}, u32[]{:S(2)}, u32[]{:S(2)}) collective-permute-start(bf16[2,16,48,384]{3,2,1,0:T(8,128)(2,1)S(1)} %get-tuple-element.194), channel_id=1, source_target_pairs={{0,1},{1,2},{2,3},{3,4},{4,5},{5,6},{6,7},{7,8},{8,9},{9,10},{10,1... | collective-permute-start | bytes 3538952 | tf_op jit(solution)/shard_map/ppermute | solution.py:22
  345.0 56.9 %collective-permute-start.10 = (bf16[2,16,48,384]{3,2,1,0:T(8,128)(2,1)}, bf16[2,16,48,384]{3,2,1,0:T(8,128)(2,1)}, u32[]{:S(2)}, u32[]{:S(2)}) collective-permute-start(bf16[2,16,48,384]{3,2,1,0:T(8,128)(2,1)} %get-tuple-element.193), channel_id=1, source_target_pairs={{1,0},{2,1},{3,2},{4,3},{5,4},{6,5},{7,6},{8,7},{9,8},{10,9},{11,1... | collective-permute-start | bytes 3538952 | tf_op jit(solution)/shard_map/ppermute | solution.py:23
  349.6 87.3 %collective-permute-start.6 = (bf16[2,16,48,384]{3,2,1,0:T(8,128)(2,1)}, bf16[2,16,48,384]{3,2,1,0:T(8,128)(2,1)}, u32[]{:S(2)}, u32[]{:S(2)}) collective-permute-start(bf16[2,16,48,384]{3,2,1,0:T(8,128)(2,1)} %get-tuple-element.192), channel_id=1, source_target_pairs={{0,1},{1,2},{2,3},{3,4},{4,5},{5,6},{6,7},{7,8},{8,9},{9,10},{10,1... | collective-permute-start | bytes 3538952 | tf_op jit(solution)/shard_map/ppermute | solution.py:22
  354.6 86.4 %collective-permute-start.7 = (bf16[2,16,48,384]{3,2,1,0:T(8,128)(2,1)}, bf16[2,16,48,384]{3,2,1,0:T(8,128)(2,1)}, u32[]{:S(2)}, u32[]{:S(2)}) collective-permute-start(bf16[2,16,48,384]{3,2,1,0:T(8,128)(2,1)} %get-tuple-element.191), channel_id=1, source_target_pairs={{1,0},{2,1},{3,2},{4,3},{5,4},{6,5},{7,6},{8,7},{9,8},{10,9},{11,1... | collective-permute-start | bytes 3538952 | tf_op jit(solution)/shard_map/ppermute | solution.py:23
  545.5 5.4 copy-start.3
  668.4 5.5 copy-start.1
  793.5 5.4 copy-start.2
  931.8 49.7 %slice-start = ((s8[10752000]{0:T(1024)(128)(4,1)}), s8[4194304]{0:T(1024)(128)(4,1)S(1)}, s32[]{:S(2)}) async-start(s8[10752000]{0:T(1024)(128)(4,1)} %bitcast.294), calls=%async_computation.2 | async-start | bytes 8388608
  931.8 49.7 %slice-start.1 = ((s8[10752000]{0:T(1024)(128)(4,1)}), s8[4194304]{0:T(1024)(128)(4,1)S(1)}, s32[]{:S(2)}) async-start(s8[10752000]{0:T(1024)(128)(4,1)} %bitcast.294), calls=%async_computation.3 | async-start | bytes 8388608
  931.8 49.7 %slice-start.2 = ((s8[10752000]{0:T(1024)(128)(4,1)}), s8[2363392]{0:T(1024)(128)(4,1)S(1)}, s32[]{:S(2)}) async-start(s8[10752000]{0:T(1024)(128)(4,1)} %bitcast.294), calls=%async_computation.4 | async-start | bytes 4726784
  981.5 37.4 %copy-start.7 = (f32[15]{0:T(128)S(1)}, f32[15]{0:T(128)}, u32[]{:S(2)}) copy-start(f32[15]{0:T(128)} %get-tuple-element.98) | copy-start | bytes 184
  981.5 37.4 %copy-start.8 = (f32[15]{0:T(128)S(1)}, f32[15]{0:T(128)}, u32[]{:S(2)}) copy-start(f32[15]{0:T(128)} %get-tuple-element.99) | copy-start | bytes 184
  981.6 37.4 %copy-start.9 = (f32[15]{0:T(128)S(1)}, f32[15]{0:T(128)}, u32[]{:S(2)}) copy-start(f32[15]{0:T(128)} %get-tuple-element.100) | copy-start | bytes 184
  981.6 37.4 %copy-start.10 = (f32[15]{0:T(128)S(1)}, f32[15]{0:T(128)}, u32[]{:S(2)}) copy-start(f32[15]{0:T(128)} %get-tuple-element.101) | copy-start | bytes 184
  981.6 37.4 %copy-start.11 = (f32[15]{0:T(128)S(1)}, f32[15]{0:T(128)}, u32[]{:S(2)}) copy-start(f32[15]{0:T(128)} %get-tuple-element.102) | copy-start | bytes 184
  981.6 37.4 %copy-start.12 = (f32[15]{0:T(128)S(1)}, f32[15]{0:T(128)}, u32[]{:S(2)}) copy-start(f32[15]{0:T(128)} %get-tuple-element.103) | copy-start | bytes 184
  981.6 37.4 %copy-start.13 = (f32[15]{0:T(128)S(1)}, f32[15]{0:T(128)}, u32[]{:S(2)}) copy-start(f32[15]{0:T(128)} %get-tuple-element.104) | copy-start | bytes 184
  981.6 37.4 %copy-start.4 = (s32[4,3,1,15]{3,2,1,0:T(1,128)S(1)}, s32[4,3,1,15]{3,2,1,0:T(1,128)}, u32[]{:S(2)}) copy-start(s32[4,3,1,15]{3,2,1,0:T(1,128)} %param.5) | copy-start | bytes 2164
  981.6 52.9 %copy-start.14 = (f32[128]{0:T(128)S(1)}, f32[128]{0:T(128)}, u32[]{:S(2)}) copy-start(f32[128]{0:T(128)} %convert_reduce_fusion) | copy-start | bytes 1540
  981.6 64.4 %copy-start.6 = (s32[384]{0:T(512)S(1)}, s32[384]{0:T(512)}, u32[]{:S(2)}) copy-start(s32[384]{0:T(512)} %copy-done.5) | copy-start | bytes 4612
  1021.3 24.5 %all-to-all-start = ((f32[3,128,3]{2,0,1:T(4,128)}), f32[3,128,3]{2,0,1:T(4,128)S(1)}, u32[]{:S(2)}, u32[]{:S(2)}) async-start(f32[3,128,3]{2,0,1:T(4,128)} %copy.83), calls=%async_computation | async-start | bytes 524288 | tf_op jit(solution)/shard_map/all_to_all | solution.py:129
where the time goes:
time: 1060 us; the launch traced here: 1050 us
  local copies, waits for them, and re-layouts  641 us (60%)
  other arithmetic  234 us (22%)
  waiting for transfers between devices  117 us (11%)
  starting transfers between devices  52.9 us (5%)
    gather x270, local copies, waits for them, and re-layouts  338 us
    unnamed x60, local copies, waits for them, and re-layouts  187 us
    dot_general x4, other arithmetic, shifted(): jnp.einsum('xyz,xyz->', block_first, piece, preferred_element_type=jnp.fl...  186 us
    all_to_all x1, waiting for transfers between devices, on_device(): lax.all_to_all(send_cells.reshape(1, devices, capacity), ('tm', 'space'),...  101 us
    pad x4, local copies, waits for them, and re-layouts, widen(): return jnp.pad(frame_set, ((0, 0), (0, 0), (H, H), (H, H + spare)))  34.4 us
    gather x4, local copies, waits for them, and re-layouts, single_window(): lax.dynamic_slice(slab_first, (zero_index, y_start, z_start), (W, W, W))  30.2 us
    select_n x1, other arithmetic, on_device(): second_set = jnp.where(is_lower, partner_wide, own_wide)  27.7 us
  transfers between devices with their start and end apart: 13, of which 3 were waited for; matrix products, arithmetic and copies ran while one was open for 28% of the time, Pallas kernels for 0%

commit v1 on v0

v1 whole, which is shorter than its diff:
```python
import functools

import jax
import jax.numpy as jnp
from jax import lax
from jax.experimental import pallas as pl
from jax.experimental.pallas import tpu as pltpu
from jax.sharding import PartitionSpec as P

W = 48
H = 16
S = 24
NWIN = 15
CELLS = 128
NS = 16
NT = 8
EXT = W + 2 * H
DEPTH = 25 * 128
BF = jnp.bfloat16
F32 = jnp.float32
MESH = pl.DeviceIdType.MESH

PASS_STEPS = {2: 3, 1: 12, 0: 20}


def lane(shape):
    return lax.broadcasted_iota(jnp.int32, shape, len(shape) - 1)


def prepare_first(planes, side, w, right):
    start = S * w
    tile = start // 128
    offset = start - 128 * tile
    here = pl.ds(pl.multiple_of(128 * tile, 128), 128)
    there = pl.ds(pl.multiple_of(128 * lax.min(tile + 1, 2), 128), 128)
    c = lane((1, 1, 128))
    d = jnp.where(c >= 64, c - 64, c + 64)
    keep = [((v >= offset) & (v < offset + W), v + 128 < offset + W) for v in (c, d)]
    zero = jnp.zeros((2, W, 128), BF)
    previous = None
    for j in range(24):
        low, high = [
            jnp.where(
                keep[r][0],
                planes[side, r, 2 * j : 2 * j + 2, :, here],
                jnp.where(keep[r][1], planes[side, r, 2 * j : 2 * j + 2, :, there], zero),
            )
            for r in range(2)
        ]
        even = low[0] + high[1]
        right[48:96, j * 128 : j * 128 + 128] = even
        right[96:144, j * 128 + 128 : j * 128 + 256] = even
        right[0:48, j * 128 : j * 128 + 128] = high[0] if previous is None else high[0] + previous
        previous = low[1]
    right[0:48, 24 * 128 :] = previous


def prepare_second(wide, side, w, qx, qz, left):
    start = S * w
    base = start - 128 * (start // 128)
    tile = (start + 112) // 128
    offset = start + qz - 1 - 128 * (tile - 1)
    here = pl.ds(pl.multiple_of(128 * lax.rem(tile + 3, 4), 128), 128)
    there = pl.ds(pl.multiple_of(128 * tile, 128), 128)
    c = lane((1, 128))
    first = c >= offset
    slot = lax.rem(c + 128 - base, 128) < 64
    turn = base - offset + 512
    for j in range(25):
        pair = [
            jnp.where(
                first,
                wide[side, H - 1 + qx + 2 * j + i, :, here],
                wide[side, H - 1 + qx + 2 * j + i, :, there],
            )
            for i in range(2)
        ]
        for e in range(3):
            left[48 * e : 48 * e + 48, j * 128 : j * 128 + 128] = jnp.where(
                slot,
                pltpu.roll(pair[0], lax.rem(turn - e, 128), 1),
                pltpu.roll(pair[1], lax.rem(turn + 64 - e, 128), 1),
            )


def correlate(left, right, qy, row, sums):
    c = lax.dot_general(left[...], right[...], (((1,), (1,)), ((), ())), preferred_element_type=F32)
    column = lax.broadcasted_iota(jnp.int32, (W, 144), 1)
    y = jnp.where(column < 48, column, jnp.where(column < 96, column - 48, column - 96))
    lag = lax.broadcasted_iota(jnp.int32, (W, 144), 0) - y - qy

    def diagonal(values, at):
        return jnp.sum(jnp.where(lag == at, values, 0.0), axis=0, keepdims=True)

    def narrow(values, at):
        return jnp.sum(
            jnp.where(lag[:, :128] == at, values[:, :128], 0.0), axis=0, keepdims=True
        )

    centre = diagonal(c[48:96], 0)
    sums[0, pl.ds(row, 1), :] = centre[:, :128]
    sums[1, pl.ds(row, 1), 0:16] = centre[:, 128:144]
    sums[2, pl.ds(row, 1), :] = narrow(c[48:96], -1)
    sums[3, pl.ds(row, 1), :] = narrow(c[48:96], 1)
    sums[4, pl.ds(row, 1), :] = narrow(c[0:48], 0)
    sums[5, pl.ds(row, 1), :] = narrow(c[96:144], 0)


def velocities(sums, peaks):
    c = lane((64, 128))

    def total(k, low, high):
        return jnp.sum(jnp.where((c >= low) & (c < high), sums[k], 0.0), axis=1, keepdims=True)

    columns = (
        total(0, 0, 48),
        total(0, 48, 96),
        total(0, 96, 128) + total(1, 0, 16),
        total(2, 0, 48),
        total(3, 0, 48),
        total(4, 0, 48),
        total(5, 0, 48),
    )
    table = jnp.zeros((64, 128), F32)
    for k, column in enumerate(columns):
        table = jnp.where(c == k, column, table)
    table = jnp.concatenate([table, table], axis=0).T * float(W) ** -1.5
    centre = table[0:1]
    each = lane((1, 128))
    gap = lax.rem(each, 64) // 16
    scale = jnp.where(gap == 0, 1.0, jnp.where(gap == 1, 0.5, jnp.where(gap == 2, 0.25, 0.125)))
    out = jnp.zeros((8, 128), F32)
    row = lax.broadcasted_iota(jnp.int32, (8, 128), 0)
    for axis in range(3):
        lower, upper = table[1 + 2 * axis : 2 + 2 * axis], table[2 + 2 * axis : 3 + 2 * axis]
        curvature = jnp.maximum(2.0 * centre - upper - lower, 1.0)
        value = (peaks[axis : axis + 1].astype(F32) + 0.5 * (upper - lower) / curvature) * scale
        out = jnp.where(row == axis, value, out)
    return jnp.where(row == 3, 1.0, out)


def kernel(
    frames, meta, velocity_out, tile_out,
    F, wide, planes, left0, left1, right0, right1, sums, hot,
    metas, mine, scalars, keys, vector, vectors, beside, parts, arrived,
    local_sem, xs, xr, cs, cr, hs, hr, ms, mr, ss, ks, kr, vs, vr, bs, br, ps, pr,
):
    tm, s = lax.axis_index("tm"), lax.axis_index("space")
    x, core = tm // 2, lax.rem(tm, 2)
    east = 2 * lax.rem(x + 1, 4) + core
    west = 2 * lax.rem(x + 3, 4) + core
    twin = 2 * x + 1 - core
    tiles = [slice(128 * k, 128 * k + 128) for k in range(3)]

    def local(i):
        return pltpu.make_async_copy(frames.at[i], F.at[i, H : H + W], local_sem.at[i])

    for i in range(2):
        local(i).start()

    barrier = pltpu.get_barrier_semaphore()
    greeted = [(tm, lax.rem(s + o, NS)) for o in range(1, NS)]
    greeted += [(lax.rem(tm + o, NT), s) for o in range(1, NT)]
    greeted += [(twin, lax.rem(s + 1, NS)), (twin, lax.rem(s + NS - 1, NS))]
    for device in greeted:
        pl.semaphore_signal(barrier, inc=1, device_id=device, device_id_type=MESH)
    pl.semaphore_wait(barrier, len(greeted))

    def remote(src, dst, send, recv, device):
        return pltpu.make_async_remote_copy(
            src_ref=src, dst_ref=dst, send_sem=send, recv_sem=recv, device_id=device, device_id_type=MESH
        )

    to_east = jnp.where(x < 2, 0, 1)

    def across(side, k):
        frame = to_east if side == 0 else 1 - to_east
        return remote(
            frames.at[frame, :, :, tiles[k]],
            F.at[3 + side, H : H + W, :, tiles[k]],
            xs.at[side, k],
            xr.at[side, k],
            (east if side == 0 else west, s),
        )

    def over():
        return remote(frames.at[1 - core], F.at[2, H : H + W], cs, cr, (twin, s))

    def halo(source, lead, slot, k, way, device_tm):
        low = lead + W - H if way == 0 else lead
        to = 0 if way == 0 else H + W
        return remote(
            source.at[pl.ds(low, H), :, tiles[k]],
            F.at[slot, to : to + H, :, tiles[k]],
            hs.at[slot, way, k],
            hr.at[slot, way, k],
            (device_tm, s + 1 if way == 0 else s - 1),
        )

    has_next = [s < NS - 1, s > 0]
    has_from = [s > 0, s < NS - 1]

    def start_halo(source, lead, slot, k, device_tm, when=None):
        for way in range(2):
            ok = has_next[way] if when is None else has_next[way] & when

            @pl.when(ok)
            def _(way=way):
                halo(source, lead, slot, k, way, device_tm).start()

    def end_halo(source, lead, slot, k, device_tm, when=None):
        for way in range(2):
            ok = has_next[way] if when is None else has_next[way] & when

            @pl.when(ok)
            def _(way=way):
                halo(source, lead, slot, k, way, device_tm).wait_send()

    def got_halo(slot, k, when=None):
        for way in range(2):
            ok = has_from[way] if when is None else has_from[way] & when

            @pl.when(ok)
            def _(way=way):
                halo(F.at[slot], H, slot, k, way, tm).wait_recv()

    own = [frames.at[0], frames.at[1]]
    for side, device in enumerate((east, west)):
        remote(meta, metas.at[side], ms.at[side], mr.at[side], (device, s)).start()
    for k in (2, 1, 0):
        start_halo(own[1], 0, 1, k, tm)
        for side in range(2):
            across(side, k).start()
    over().start()
    for k in (2, 1, 0):
        start_halo(own[0], 0, 2, k, twin, core == 1)
        start_halo(own[0], 0, 0, k, tm, x == 1)

    @pl.when(s == 0)
    def _():
        for slot in range(5):
            F[slot, 0:H] = jnp.zeros((H, W, 384), BF)

    @pl.when(s == NS - 1)
    def _():
        for slot in range(5):
            F[slot, H + W :] = jnp.zeros((H, W, 384), BF)

    wide[:, :, :, 384:] = jnp.zeros((2, EXT, W, 128), BF)
    for right in (right0, right1):
        right[48:96, 24 * 128 :] = jnp.zeros((W, 128), BF)
        right[96:144, 0:128] = jnp.zeros((W, 128), BF)
    sums[...] = jnp.zeros_like(sums)

    for side in range(2):
        remote(meta, metas.at[side], ms.at[side], mr.at[side], (east, s)).wait()
    gap = lax.rem(lane((8, 128)), 64) // 16
    third = jnp.where(x == 0, metas[1], jnp.where(x == 1, metas[0], meta[...]))
    mine[...] = jnp.where(gap < 2, meta[...], jnp.where(gap == 2, third, metas[0]))
    to_scalars = pltpu.make_async_copy(mine, scalars, ss)
    to_scalars.start()

    def key_copy(o):
        return remote(mine, keys.at[s], ks.at[o - 1], kr.at[o - 1], (tm, lax.rem(s + o, NS)))

    for o in range(1, NS):
        key_copy(o).start()
    keys[s] = mine[...]
    to_scalars.wait()

    def by_x(a, b, c, d):
        return jnp.where(x == 0, a, jnp.where(x == 1, b, jnp.where(x == 2, c, d)))

    firsts = [0, jnp.where(core == 0, 0, 2), by_x(1, 3, 0, 3), by_x(4, 3, 3, 4)]
    seconds = [1, jnp.where(core == 0, 2, 1), by_x(4, 0, 4, 1), by_x(3, 4, 4, 3)]

    def stage(pair, k):
        first, second, side = firsts[pair], seconds[pair], pair % 2

        def put(b, _):
            at = pl.ds(8 * b, 8)
            part = F[first, pl.ds(H + 8 * b, 8), :, tiles[k]]
            planes[side, 0, at, :, tiles[k]] = part
            planes[side, 1, at, :, tiles[k]] = pltpu.roll(part, 64, 2)
            return 0

        lax.fori_loop(0, W // 8, put, 0)

        def fill(b, _):
            at = pl.ds(16 * b, 16)
            wide[side, at, :, tiles[k]] = F[second, at, :, tiles[k]]
            return 0

        lax.fori_loop(0, EXT // 16, fill, 0)

    def stage_own(k):
        if k == 2:
            for i in range(2):
                local(i).wait()
        got_halo(1, k)
        stage(0, k)

    def stage_twin(k):
        if k == 2:
            over().wait_recv()
        got_halo(2, k, core == 0)
        stage(1, k)

    def pass_on(k):
        for side in range(2):
            across(side, k).wait_recv()
        for slot in (3, 4):
            uses = (x == 0) | (x == 3) if slot == 3 else x < 3
            start_halo(F.at[slot], H, slot, k, tm, uses)

    def stage_across(k):
        got_halo(0, k, x == 1)
        got_halo(3, k, (x == 0) | (x == 3))
        got_halo(4, k, x < 3)
        stage(2, k)
        stage(3, k)

    def item(i):
        late = i - 30
        pair = jnp.where(i < 15, 0, jnp.where(i < 30, 1, 2 + lax.rem(late + 30, 2)))
        w = jnp.where(i < 15, 14 - i, jnp.where(i < 30, 29 - i, 14 - (late + 30) // 2 + 15))
        return pair, w

    def prepare(i, left, right):
        pair, w = item(i)
        at = 16 * pair + w
        side = lax.rem(pair, 2)
        prepare_first(planes, side, w, right)
        prepare_second(wide, side, w, scalars[0, at], scalars[2, at], left)

    def finish(i, left, right):
        pair, w = item(i)
        at = 16 * pair + w
        correlate(left, right, scalars[1, at], at, sums)

    stage_own(2)
    prepare(0, left0, right0)
    events = {1: (stage_own, 1), 4: (stage_own, 0), 7: (stage_twin, 2), 8: (stage_twin, 1), 11: (stage_twin, 0)}
    events.update({14: (stage_across, 2), 17: (stage_across, 1), 23: (stage_across, 0)})

    def step(h, _):
        for k, at in PASS_STEPS.items():

            @pl.when(h == at)
            def _(k=k):
                pass_on(k)

        for at, (event, k) in events.items():

            @pl.when(h == at)
            def _(event=event, k=k):
                event(k)

        prepare(2 * h + 1, left1, right1)
        finish(2 * h, left0, right0)
        prepare(lax.min(2 * h + 2, 59), left0, right0)
        finish(2 * h + 1, left1, right1)
        return 0

    for o in range(1, NS):
        key_copy(o).wait()
    for pair in range(NS // 2):
        key = jnp.where(lane((1, 128)) < 64, keys[2 * pair, 3:4], keys[2 * pair + 1, 3:4])
        owner = key // CELLS
        cell = key - owner * CELLS
        there = owner // NS
        row = jnp.where((key >= 0) & (owner - there * NS == s), there * CELLS + cell, -1)

        def put(t, _, pair=pair, row=row):
            number = CELLS * t + lax.broadcasted_iota(jnp.int32, (CELLS, 128), 0)
            hot[pl.ds(pl.multiple_of(CELLS * t, CELLS), CELLS), 128 * pair : 128 * pair + 128] = jnp.where(
                number == row, 1.0, 0.0
            ).astype(BF)
            return 0

        lax.fori_loop(0, NT, put, 0)

    lax.fori_loop(0, 30, step, 0)

    values = velocities(sums, mine[...])
    vector[...] = values

    def vector_copy(o):
        return remote(vector, vectors.at[s], vs.at[o - 1], vr.at[o - 1], (tm, lax.rem(s + o, NS)))

    def vector_beside(side):
        return remote(vector, beside.at[side], bs.at[side], br.at[side], (east if side == 0 else west, s))

    for o in range(1, NS):
        vector_copy(o).start()
    for side in range(2):
        vector_beside(side).start()
    vectors[s] = values
    for o in range(1, NS):
        vector_copy(o).wait_recv()
    rows = jnp.concatenate(
        [
            jnp.where(lane((8, 128)) < 64, vectors[2 * pair], vectors[2 * pair + 1])
            for pair in range(NS // 2)
        ],
        axis=1,
    )
    high = rows.astype(BF).astype(F32)
    middle = (rows - high).astype(BF).astype(F32)
    low = rows - high - middle
    split = jnp.concatenate([high, middle, low, jnp.zeros_like(low)], axis=0).astype(BF)
    cell_sums = lax.dot_general(split, hot[...], (((1,), (1,)), ((), ())), preferred_element_type=F32)
    cell_sums = cell_sums[0:8] + cell_sums[8:16] + cell_sums[16:24]
    for t in range(NT):
        parts[t] = cell_sums[:, CELLS * t : CELLS * t + CELLS]

    def part_copy(o):
        to = lax.rem(tm + o, NT)
        return remote(parts.at[to], arrived.at[tm], ps.at[o - 1], pr.at[o - 1], (to, s))

    for o in range(1, NT):
        part_copy(o).start()
    arrived[tm] = parts[tm]

    for side in range(2):
        vector_beside(side).wait()
    gap = lax.rem(lane((8, 128)), 64) // 16
    third = jnp.where(x == 0, beside[1], jnp.where(x == 1, beside[0], values))
    velocity_out[...] = jnp.where(gap < 2, values, jnp.where(gap == 2, third, beside[1]))

    for o in range(1, NS):
        vector_copy(o).wait_send()
    over().wait_send()
    for k in range(3):
        for side in range(2):
            across(side, k).wait_send()
        end_halo(own[1], 0, 1, k, tm)
        end_halo(own[0], 0, 2, k, twin, core == 1)
        end_halo(own[0], 0, 0, k, tm, x == 1)
        end_halo(F.at[3], H, 3, k, tm, (x == 0) | (x == 3))
        end_halo(F.at[4], H, 4, k, tm, x < 3)

    for o in range(1, NT):
        part_copy(o).wait()
    total = arrived[0]
    for t in range(1, NT):
        total = total + arrived[t]
    tile_out[...] = total / jnp.maximum(total[3:4], 1.0)


def on_device(frames, peak_voxels, owners, tile_cells):
    peaks = jnp.transpose(peak_voxels[:, :, 0, :], (1, 0, 2))
    peaks = jnp.pad(peaks, ((0, 0), (0, 0), (0, 1))).reshape(3, 64)
    key = (owners[:, 0] * CELLS + tile_cells).reshape(4, NWIN)
    key = jnp.pad(key, ((0, 0), (0, 1)), constant_values=-1).reshape(1, 64)
    meta = jnp.pad(jnp.concatenate([peaks, key], axis=0), ((0, 4), (0, 0)))
    meta = jnp.concatenate([meta, meta], axis=1)
    dma = pltpu.SemaphoreType.DMA
    vmem = pltpu.VMEM
    velocity, tile = pl.pallas_call(
        kernel,
        out_shape=[jax.ShapeDtypeStruct((8, 128), F32)] * 2,
        in_specs=[pl.BlockSpec(memory_space=pltpu.HBM), pl.BlockSpec(memory_space=vmem)],
        out_specs=[pl.BlockSpec(memory_space=vmem)] * 2,
        scratch_shapes=[
            vmem((5, EXT, W, 384), BF),
            vmem((2, EXT, W, 512), BF),
            vmem((2, 2, W, W, 384), BF),
            vmem((144, DEPTH), BF),
            vmem((144, DEPTH), BF),
            vmem((144, DEPTH), BF),
            vmem((144, DEPTH), BF),
            vmem((6, 64, 128), F32),
            vmem((NT * CELLS, NS * 64), BF),
            vmem((2, 8, 128), jnp.int32),
            vmem((8, 128), jnp.int32),
            pltpu.SMEM((8, 128), jnp.int32),
            vmem((NS, 8, 128), jnp.int32),
            vmem((8, 128), F32),
            vmem((NS, 8, 128), F32),
            vmem((2, 8, 128), F32),
            vmem((NT, 8, 128), F32),
            vmem((NT, 8, 128), F32),
            dma((2,)),
            dma((2, 3)),
            dma((2, 3)),
            dma,
            dma,
            dma((5, 2, 3)),
            dma((5, 2, 3)),
            dma((2,)),
            dma((2,)),
            dma,
            dma((NS - 1,)),
            dma((NS - 1,)),
            dma((NS - 1,)),
            dma((NS - 1,)),
            dma((2,)),
            dma((2,)),
            dma((NT - 1,)),
            dma((NT - 1,)),
        ],
        compiler_params=pltpu.CompilerParams(
            collective_id=0, has_side_effects=True, vmem_limit_bytes=56 * 2**20
        ),
    )(frames, meta)
    velocity = velocity[:3, :64].reshape(3, 4, 16)[:, :, :NWIN]
    return jnp.transpose(velocity, (1, 0, 2))[:, :, None, :], tile[:3]


def solution(mesh):
    placed = (
        P("tm", "space", None, None),
        P(None, None, "tm", "space"),
        P(("tm", "space"), None),
        P(("tm", "space")),
    )
    return jax.shard_map(
        on_device,
        mesh=mesh,
        in_specs=placed,
        out_specs=(P(None, None, "tm", "space"), P(None, ("tm", "space"))),
        check_vma=False,
    )
```

time: 1060 us -> 123 us (0.12); the launches traced: 1050 us -> 123 us
  local copies, waits for them, and re-layouts: 641 us -> 3.59 us
  other arithmetic: 234 us -> 1.36 us
  Pallas kernels: 0 us -> 117 us
  waiting for transfers between devices: 117 us -> 0 us
  starting transfers between devices: 52.9 us -> 0 us
    gather x278 -> x0, local copies, waits for them, and re-layouts: 370 us -> none
    dot_general x4 -> x0, other arithmetic: 186 us -> none  [shifted(): jnp.einsum('xyz,xyz->', block_first, piece, preferred_element_type=jnp.fl...]
    unnamed x60 -> x2, local copies, waits for them, and re-layouts: 187 us -> 1.3 us
    pallas_call x0 -> x1, Pallas kernels: none -> 117 us  [on_device(): pl.pallas_call(kernel, out_shape=[jax.ShapeDtypeStruct((8, 128), F32)] *...]
    all_to_all x2 -> x0, waiting for transfers between devices: 112 us -> none  [the longest x1 101 us: on_device(): lax.all_to_all(send_cells.reshape(1, devices, capacity), ('tm', 'space'),...]
    select_n x4 -> x0, other arithmetic: 41.5 us -> none  [the longest x1 27.7 us: on_device(): second_set = jnp.where(is_lower, partner_wide, own_wide)]
    pad x4 -> x3, local copies, waits for them, and re-layouts: 34.4 us -> 0.02 us  [the longest x1 0.01 us: on_device(): key = jnp.pad(key, ((0, 0), (0, 1)), constant_values=-1).reshape(1, 64)]
    ppermute x11 -> x0, starting transfers between devices: 27.1 us -> none  [the longest x4 16.7 us: extended(): before = lax.ppermute(last, axis, up)]
  transfers between devices with their start and end apart: 13 -> 0, of which waited for: 3 -> 0; matrix products, arithmetic and copies ran while one was open for 28% -> 0% of each run, Pallas kernels for 0% -> 0%
where the time goes in v1:
time: 123 us
  Pallas kernels  117 us (95%)
  local copies, waits for them, and re-layouts  3.59 us (3%)
  other arithmetic  1.36 us (1%)
    pallas_call x1, Pallas kernels, on_device(): pl.pallas_call(kernel, out_shape=[jax.ShapeDtypeStruct((8, 128), F32)] *...  117 us

profile of v1, /device:TPU:1, one launch (start us, length us, event | category | flops | bytes accessed | tf_op | source)
XLA Modules:
  0.0 122.9 jit_solution(2294467132513239917)
XLA Ops:
  0.6 0.7 bitcast_add_fusion
  1.3 0.1 reshape.19
  1.4 0.1 reshape.20
  1.5 0.7 copy.11
  2.2 0.1 reshape.18
  2.3 0.7 pad_add_fusion.meta
  3.0 117.3 %shard_map.59 = (f32[8,128]{1,0:T(8,128)}, f32[8,128]{1,0:T(8,128)}) custom-call(bf16[2,48,48,384]{3,2,1,0:T(8,128)(2,1)} %frames.1, s32[8,128]{1,0:T(8,128)} %pad_add_fusion.meta), custom_call_target="tpu_custom_call" | custom-call | tf_op jit(solution)/shard_map/pallas_call | solution.py:460
  120.3 0.7 slice.9
  120.9 1.2 %slice.11 = f32[3,128]{1,0:T(4,128)} slice(f32[8,128]{1,0:T(8,128)} %get-tuple-element.5), slice={[0:3], [0:128]} | slice | bytes 3072 | tf_op jit(solution)/shard_map/slice | solution.py:508
  122.2 0.1 reshape.21
  122.3 0.6 copy.9
  (5 shorter events, 0.0 us)

commit v2 on v1

--- a/solution.py
+++ b/solution.py
@@ -20,7 +20,7 @@
 F32 = jnp.float32
 MESH = pl.DeviceIdType.MESH
 
-PASS_STEPS = {2: 3, 1: 12, 0: 20}
+PASS_STEPS = {2: 9, 1: 14, 0: 20}
 
 
 def lane(shape):
@@ -63,23 +63,18 @@
     here = pl.ds(pl.multiple_of(128 * lax.rem(tile + 3, 4), 128), 128)
     there = pl.ds(pl.multiple_of(128 * tile, 128), 128)
     c = lane((1, 128))
-    first = c >= offset
-    slot = lax.rem(c + 128 - base, 128) < 64
+    d = jnp.where(c >= 64, c - 64, c + 64)
+    first, first_turned = c >= offset, d >= offset
+    slot = lax.rem(c + 256 - offset, 128) < 64
     turn = base - offset + 512
     for j in range(25):
-        pair = [
-            jnp.where(
-                first,
-                wide[side, H - 1 + qx + 2 * j + i, :, here],
-                wide[side, H - 1 + qx + 2 * j + i, :, there],
-            )
-            for i in range(2)
-        ]
+        x = H - 1 + qx + 2 * j
+        even = jnp.where(first, wide[side, 0, x, :, here], wide[side, 0, x, :, there])
+        odd = jnp.where(first_turned, wide[side, 1, x + 1, :, here], wide[side, 1, x + 1, :, there])
+        pair = jnp.where(slot, even, odd)
         for e in range(3):
-            left[48 * e : 48 * e + 48, j * 128 : j * 128 + 128] = jnp.where(
-                slot,
-                pltpu.roll(pair[0], lax.rem(turn - e, 128), 1),
-                pltpu.roll(pair[1], lax.rem(turn + 64 - e, 128), 1),
+            left[48 * e : 48 * e + 48, j * 128 : j * 128 + 128] = pltpu.roll(
+                pair, lax.rem(turn - e, 128), 1
             )
 
 
@@ -157,6 +152,7 @@
 
     for i in range(2):
         local(i).start()
+    pltpu.make_async_copy(meta, scalars, ss).start()
 
     barrier = pltpu.get_barrier_semaphore()
     greeted = [(tm, lax.rem(s + o, NS)) for o in range(1, NS)]
@@ -225,16 +221,17 @@
                 halo(F.at[slot], H, slot, k, way, tm).wait_recv()
 
     own = [frames.at[0], frames.at[1]]
-    for side, device in enumerate((east, west)):
-        remote(meta, metas.at[side], ms.at[side], mr.at[side], (device, s)).start()
+
+    def meta_copy(side):
+        return remote(meta, metas.at[side], ms.at[side], mr.at[side], (east if side == 0 else west, s))
+
+    start_halo(own[1], 0, 1, 2, tm)
     for k in (2, 1, 0):
-        start_halo(own[1], 0, 1, k, tm)
         for side in range(2):
             across(side, k).start()
     over().start()
-    for k in (2, 1, 0):
-        start_halo(own[0], 0, 2, k, twin, core == 1)
-        start_halo(own[0], 0, 0, k, tm, x == 1)
+    for side in range(2):
+        meta_copy(side).start()
 
     @pl.when(s == 0)
     def _():
@@ -246,27 +243,31 @@
         for slot in range(5):
             F[slot, H + W :] = jnp.zeros((H, W, 384), BF)
 
-    wide[:, :, :, 384:] = jnp.zeros((2, EXT, W, 128), BF)
+    wide[:, :, :, :, 384:] = jnp.zeros((2, 2, EXT, W, 128), BF)
     for right in (right0, right1):
         right[48:96, 24 * 128 :] = jnp.zeros((W, 128), BF)
         right[96:144, 0:128] = jnp.zeros((W, 128), BF)
     sums[...] = jnp.zeros_like(sums)
 
-    for side in range(2):
-        remote(meta, metas.at[side], ms.at[side], mr.at[side], (east, s)).wait()
-    gap = lax.rem(lane((8, 128)), 64) // 16
-    third = jnp.where(x == 0, metas[1], jnp.where(x == 1, metas[0], meta[...]))
-    mine[...] = jnp.where(gap < 2, meta[...], jnp.where(gap == 2, third, metas[0]))
-    to_scalars = pltpu.make_async_copy(mine, scalars, ss)
-    to_scalars.start()
+    end_halo(own[1], 0, 1, 2, tm)
+    for k in (1, 0):
+        start_halo(own[1], 0, 1, k, tm)
 
     def key_copy(o):
         return remote(mine, keys.at[s], ks.at[o - 1], kr.at[o - 1], (tm, lax.rem(s + o, NS)))
 
-    for o in range(1, NS):
-        key_copy(o).start()
-    keys[s] = mine[...]
-    to_scalars.wait()
+    def share_keys():
+        for side in range(2):
+            meta_copy(side).wait()
+        gap = lax.rem(lane((8, 128)), 64) // 16
+        third = jnp.where(x == 0, metas[1], jnp.where(x == 1, metas[0], meta[...]))
+        mine[...] = jnp.where(gap < 2, meta[...], jnp.where(gap == 2, third, metas[0]))
+        to_scalars = pltpu.make_async_copy(mine, scalars, ss)
+        to_scalars.start()
+        for o in range(1, NS):
+            key_copy(o).start()
+        keys[s] = mine[...]
+        to_scalars.wait()
 
     def by_x(a, b, c, d):
         return jnp.where(x == 0, a, jnp.where(x == 1, b, jnp.where(x == 2, c, d)))
@@ -274,51 +275,63 @@
     firsts = [0, jnp.where(core == 0, 0, 2), by_x(1, 3, 0, 3), by_x(4, 3, 3, 4)]
     seconds = [1, jnp.where(core == 0, 2, 1), by_x(4, 0, 4, 1), by_x(3, 4, 4, 3)]
 
+    def mark_cells():
+        for o in range(1, NS):
+            key_copy(o).wait()
+        for pair in range(NS // 2):
+            key = jnp.where(lane((1, 128)) < 64, keys[2 * pair, 3:4], keys[2 * pair + 1, 3:4])
+            owner = key // CELLS
+            cell = key - owner * CELLS
+            there = owner // NS
+            row = jnp.where((key >= 0) & (owner - there * NS == s), there * CELLS + cell, -1)
+
+            def put(t, _, pair=pair, row=row):
+                number = CELLS * t + lax.broadcasted_iota(jnp.int32, (CELLS, 128), 0)
+                hot[pl.ds(pl.multiple_of(CELLS * t, CELLS), CELLS), 128 * pair : 128 * pair + 128] = jnp.where(
+                    number == row, 1.0, 0.0
+                ).astype(BF)
+                return 0
+
+            lax.fori_loop(0, NT, put, 0)
+
     def stage(pair, k):
-        first, second, side = firsts[pair], seconds[pair], pair % 2
-
-        def put(b, _):
-            at = pl.ds(8 * b, 8)
-            part = F[first, pl.ds(H + 8 * b, 8), :, tiles[k]]
-            planes[side, 0, at, :, tiles[k]] = part
-            planes[side, 1, at, :, tiles[k]] = pltpu.roll(part, 64, 2)
-            return 0
-
-        lax.fori_loop(0, W // 8, put, 0)
-
-        def fill(b, _):
-            at = pl.ds(16 * b, 16)
-            wide[side, at, :, tiles[k]] = F[second, at, :, tiles[k]]
-            return 0
-
-        lax.fori_loop(0, EXT // 16, fill, 0)
-
-    def stage_own(k):
-        if k == 2:
-            for i in range(2):
-                local(i).wait()
-        got_halo(1, k)
-        stage(0, k)
-
-    def stage_twin(k):
+        first, second, side = firsts[3], seconds[3], lax.rem(pair, 2)
+        for p in range(3):
+            first = jnp.where(pair == p, firsts[p], first)
+            second = jnp.where(pair == p, seconds[p], second)
+        at = pl.ds(pl.multiple_of(128 * k, 128), 128)
+        for b in range(0, W, 8):
+            part = F[first, H + b : H + b + 8, :, at]
+            planes[side, 0, b : b + 8, :, at] = part
+            planes[side, 1, b : b + 8, :, at] = pltpu.roll(part, 64, 2)
+        for b in range(0, EXT, 8):
+            part = F[second, b : b + 8, :, at]
+            wide[side, 0, b : b + 8, :, at] = part
+            wide[side, 1, b : b + 8, :, at] = pltpu.roll(part, 64, 2)
+
+    def pass_on(k):
+        for side in range(2):
+            across(side, k).wait_recv()
+        start_halo(own[0], 0, 0, k, tm, x == 1)
+        for slot in (3, 4):
+            uses = (x == 0) | (x == 3) if slot == 3 else x < 3
+            start_halo(F.at[slot], H, slot, k, tm, uses)
+
+    def twin_halos():
+        for k in (1, 0):
+            end_halo(own[1], 0, 1, k, tm)
+        for k in (2, 1, 0):
+            start_halo(own[0], 0, 2, k, twin, core == 1)
+
+    def got_twin(k):
         if k == 2:
             over().wait_recv()
         got_halo(2, k, core == 0)
-        stage(1, k)
-
-    def pass_on(k):
-        for side in range(2):
-            across(side, k).wait_recv()
-        for slot in (3, 4):
-            uses = (x == 0) | (x == 3) if slot == 3 else x < 3
-            start_halo(F.at[slot], H, slot, k, tm, uses)
-
-    def stage_across(k):
+
+    def got_across(k):
         got_halo(0, k, x == 1)
         got_halo(3, k, (x == 0) | (x == 3))
         got_halo(4, k, x < 3)
-        stage(2, k)
-        stage(3, k)
 
     def item(i):
         late = i - 30
@@ -338,47 +351,46 @@
         at = 16 * pair + w
         correlate(left, right, scalars[1, at], at, sums)
 
-    stage_own(2)
+    for i in range(2):
+        local(i).wait()
+    got_halo(1, 2)
+    pltpu.make_async_copy(meta, scalars, ss).wait()
+    stage(0, 2)
     prepare(0, left0, right0)
-    events = {1: (stage_own, 1), 4: (stage_own, 0), 7: (stage_twin, 2), 8: (stage_twin, 1), 11: (stage_twin, 0)}
-    events.update({14: (stage_across, 2), 17: (stage_across, 1), 23: (stage_across, 0)})
+    events = [
+        (1, functools.partial(got_halo, 1, 1)),
+        (2, share_keys),
+        (3, twin_halos),
+        (4, functools.partial(got_halo, 1, 0)),
+        (5, mark_cells),
+        (7, functools.partial(got_twin, 2)),
+        (8, functools.partial(got_twin, 1)),
+        (11, functools.partial(got_twin, 0)),
+    ]
+    events += [(at, functools.partial(pass_on, k)) for k, at in PASS_STEPS.items()]
+    events += [(at, functools.partial(got_across, k)) for k, at in ((2, 14), (1, 17), (0, 23))]
 
     def step(h, _):
-        for k, at in PASS_STEPS.items():
-
-            @pl.when(h == at)
-            def _(k=k):
-                pass_on(k)
-
-        for at, (event, k) in events.items():
-
-            @pl.when(h == at)
-            def _(event=event, k=k):
-                event(k)
+        for at, event in events:
+            pl.when(h == at)(event)
+
+        @pl.when((h == 1) | (h == 4) | (h == 7) | (h == 8) | (h == 11))
+        def _():
+            stage(jnp.where(h < 7, 0, 1), jnp.where(h == 7, 2, jnp.where((h == 1) | (h == 8), 1, 0)))
+
+        @pl.when((h == 14) | (h == 17) | (h == 23))
+        def _():
+            def both(pair, _):
+                stage(pair, jnp.where(h == 14, 2, jnp.where(h == 17, 1, 0)))
+                return 0
+
+            lax.fori_loop(2, 4, both, 0)
 
         prepare(2 * h + 1, left1, right1)
         finish(2 * h, left0, right0)
         prepare(lax.min(2 * h + 2, 59), left0, right0)
         finish(2 * h + 1, left1, right1)
         return 0
-
-    for o in range(1, NS):
-        key_copy(o).wait()
-    for pair in range(NS // 2):
-        key = jnp.where(lane((1, 128)) < 64, keys[2 * pair, 3:4], keys[2 * pair + 1, 3:4])
-        owner = key // CELLS
-        cell = key - owner * CELLS
-        there = owner // NS
-        row = jnp.where((key >= 0) & (owner - there * NS == s), there * CELLS + cell, -1)
-
-        def put(t, _, pair=pair, row=row):
-            number = CELLS * t + lax.broadcasted_iota(jnp.int32, (CELLS, 128), 0)
-            hot[pl.ds(pl.multiple_of(CELLS * t, CELLS), CELLS), 128 * pair : 128 * pair + 128] = jnp.where(
-                number == row, 1.0, 0.0
-            ).astype(BF)
-            return 0
-
-        lax.fori_loop(0, NT, put, 0)
 
     lax.fori_loop(0, 30, step, 0)
 
@@ -426,7 +438,10 @@
         vector_beside(side).wait()
     gap = lax.rem(lane((8, 128)), 64) // 16
     third = jnp.where(x == 0, beside[1], jnp.where(x == 1, beside[0], values))
-    velocity_out[...] = jnp.where(gap < 2, values, jnp.where(gap == 2, third, beside[1]))
+    listed = jnp.where(gap < 2, values, jnp.where(gap == 2, third, beside[1]))
+    for a in range(4):
+        for i in range(3):
+            velocity_out[a, i] = pltpu.roll(listed, 128 - 16 * a, 1)[i : i + 1, :NWIN] if a else listed[i : i + 1, :NWIN]
 
     for o in range(1, NS):
         vector_copy(o).wait_send()
@@ -434,7 +449,6 @@
     for k in range(3):
         for side in range(2):
             across(side, k).wait_send()
-        end_halo(own[1], 0, 1, k, tm)
         end_halo(own[0], 0, 2, k, twin, core == 1)
         end_halo(own[0], 0, 0, k, tm, x == 1)
         end_halo(F.at[3], H, 3, k, tm, (x == 0) | (x == 3))
@@ -445,7 +459,7 @@
     total = arrived[0]
     for t in range(1, NT):
         total = total + arrived[t]
-    tile_out[...] = total / jnp.maximum(total[3:4], 1.0)
+    tile_out[...] = total[0:3] / jnp.maximum(total[3:4], 1.0)
 
 
 def on_device(frames, peak_voxels, owners, tile_cells):
@@ -459,12 +473,12 @@
     vmem = pltpu.VMEM
     velocity, tile = pl.pallas_call(
         kernel,
-        out_shape=[jax.ShapeDtypeStruct((8, 128), F32)] * 2,
+        out_shape=[jax.ShapeDtypeStruct((4, 3, 1, NWIN), F32), jax.ShapeDtypeStruct((3, CELLS), F32)],
         in_specs=[pl.BlockSpec(memory_space=pltpu.HBM), pl.BlockSpec(memory_space=vmem)],
         out_specs=[pl.BlockSpec(memory_space=vmem)] * 2,
         scratch_shapes=[
             vmem((5, EXT, W, 384), BF),
-            vmem((2, EXT, W, 512), BF),
+            vmem((2, 2, EXT, W, 512), BF),
             vmem((2, 2, W, W, 384), BF),
             vmem((144, DEPTH), BF),
             vmem((144, DEPTH), BF),
@@ -504,8 +518,7 @@
             collective_id=0, has_side_effects=True, vmem_limit_bytes=56 * 2**20
         ),
     )(frames, meta)
-    velocity = velocity[:3, :64].reshape(3, 4, 16)[:, :, :NWIN]
-    return jnp.transpose(velocity, (1, 0, 2))[:, :, None, :], tile[:3]
+    return velocity, tile
 
 
 def solution(mesh):

time: 123 us -> 128 us (1.041)
  Pallas kernels: 117 us -> 122 us
    pallas_call x1, Pallas kernels: 117 us -> 122 us  [on_device(): pl.pallas_call(kernel, out_shape=[jax.ShapeDtypeStruct((4, 3, 1, NWIN), F...]
    slice x2 -> x0, local copies, waits for them, and re-layouts: 1.92 us -> none  [the longest x1 1.25 us: on_device(): return (jnp.transpose(velocity, (1, 0, 2))[:, :, None, :], tile[:3])]
    unnamed x2 -> x3, local copies, waits for them, and re-layouts: 1.3 us -> 3.22 us
where the time goes in v2:
time: 128 us
  Pallas kernels  122 us (95%)
  local copies, waits for them, and re-layouts  3.49 us (3%)
  other arithmetic  1.36 us (1%)
    pallas_call x1, Pallas kernels, on_device(): pl.pallas_call(kernel, out_shape=[jax.ShapeDtypeStruct((4, 3, 1, NWIN), F...  122 us
    unnamed x3, local copies, waits for them, and re-layouts  3.22 us

profile of v2, /device:TPU:1, one launch (start us, length us, event | category | flops | bytes accessed | tf_op | source)
XLA Modules:
  0.0 127.6 jit_solution(7909828886212484104)
XLA Ops:
  0.6 0.7 bitcast_add_fusion
  1.3 0.1 reshape.16
  1.4 0.1 reshape.17
  1.5 0.7 copy.9
  2.2 0.1 reshape.15
  2.3 0.7 pad_add_fusion.meta
  3.0 122.1 %shard_map.59 = (f32[4,3,1,15]{3,2,1,0:T(1,128)}, f32[3,128]{1,0:T(4,128)}) custom-call(bf16[2,48,48,384]{3,2,1,0:T(8,128)(2,1)} %frames.1, s32[8,128]{1,0:T(8,128)} %pad_add_fusion.meta), custom_call_target="tpu_custom_call" | custom-call | tf_op jit(solution)/shard_map/pallas_call | solution.py:474
  125.1 1.3 %copy.12 = f32[4,3,1,15]{3,2,1,0:T(1,128)} copy(f32[4,3,1,15]{3,2,1,0:T(1,128)} %get-tuple-element.4) | data formatting | bytes 1440
  126.4 1.2 copy.13
  (4 shorter events, 0.0 us)

commit v3 on v2

--- a/solution.py
+++ b/solution.py
@@ -20,7 +20,8 @@
 F32 = jnp.float32
 MESH = pl.DeviceIdType.MESH
 
-PASS_STEPS = {2: 9, 1: 14, 0: 20}
+PASS_STEPS = {2: 6, 1: 10, 0: 15}
+SEND_STEPS = (1, 5, 9, 12)
 
 
 def lane(shape):
@@ -169,15 +170,44 @@
 
     to_east = jnp.where(x < 2, 0, 1)
 
-    def across(side, k):
+    def across(side, k, part):
         frame = to_east if side == 0 else 1 - to_east
+        low = (0, W - H, H)[part]
         return remote(
-            frames.at[frame, :, :, tiles[k]],
-            F.at[3 + side, H : H + W, :, tiles[k]],
-            xs.at[side, k],
-            xr.at[side, k],
+            frames.at[frame, low : low + H, :, tiles[k]],
+            F.at[3 + side, H + low : H + low + H, :, tiles[k]],
+            xs.at[side, k, part],
+            xr.at[side, k, part],
             (east if side == 0 else west, s),
         )
+
+    def each_across(ks, parts, act):
+        for k in ks:
+            for part in parts:
+                for side in range(2):
+                    act(across(side, k, part))
+
+    def begin(copy):
+        copy.start()
+
+    def sent(copy):
+        copy.wait_send()
+
+    def received(copy):
+        copy.wait_recv()
+
+    outer, inner = (0, 1), (2,)
+
+    def next_across(past, past_parts, ks, parts):
+        each_across(past, past_parts, sent)
+        each_across(ks, parts, begin)
+
+    sends = (
+        ((2,), outer, (1,), outer),
+        ((1,), outer, (0,), outer),
+        ((0,), outer, (2,), inner),
+        ((2,), inner, (1, 0), inner),
+    )
 
     def over():
         return remote(frames.at[1 - core], F.at[2, H : H + W], cs, cr, (twin, s))
@@ -226,9 +256,7 @@
         return remote(meta, metas.at[side], ms.at[side], mr.at[side], (east if side == 0 else west, s))
 
     start_halo(own[1], 0, 1, 2, tm)
-    for k in (2, 1, 0):
-        for side in range(2):
-            across(side, k).start()
+    each_across((2,), outer, begin)
     over().start()
     for side in range(2):
         meta_copy(side).start()
@@ -310,8 +338,7 @@
             wide[side, 1, b : b + 8, :, at] = pltpu.roll(part, 64, 2)
 
     def pass_on(k):
-        for side in range(2):
-            across(side, k).wait_recv()
+        each_across((k,), outer, received)
         start_halo(own[0], 0, 0, k, tm, x == 1)
         for slot in (3, 4):
             uses = (x == 0) | (x == 3) if slot == 3 else x < 3
@@ -329,6 +356,7 @@
         got_halo(2, k, core == 0)
 
     def got_across(k):
+        each_across((k,), inner, received)
         got_halo(0, k, x == 1)
         got_halo(3, k, (x == 0) | (x == 3))
         got_halo(4, k, x < 3)
@@ -367,6 +395,7 @@
         (8, functools.partial(got_twin, 1)),
         (11, functools.partial(got_twin, 0)),
     ]
+    events += [(at, functools.partial(next_across, *send)) for at, send in zip(SEND_STEPS, sends)]
     events += [(at, functools.partial(pass_on, k)) for k, at in PASS_STEPS.items()]
     events += [(at, functools.partial(got_across, k)) for k, at in ((2, 14), (1, 17), (0, 23))]
 
@@ -446,9 +475,8 @@
     for o in range(1, NS):
         vector_copy(o).wait_send()
     over().wait_send()
+    each_across((1, 0), inner, sent)
     for k in range(3):
-        for side in range(2):
-            across(side, k).wait_send()
         end_halo(own[0], 0, 2, k, twin, core == 1)
         end_halo(own[0], 0, 0, k, tm, x == 1)
         end_halo(F.at[3], H, 3, k, tm, (x == 0) | (x == 3))
@@ -496,8 +524,8 @@
             vmem((NT, 8, 128), F32),
             vmem((NT, 8, 128), F32),
             dma((2,)),
-            dma((2, 3)),
-            dma((2, 3)),
+            dma((2, 3, 3)),
+            dma((2, 3, 3)),
             dma,
             dma,
             dma((5, 2, 3)),

time: 128 us -> 96.9 us (0.76)
  Pallas kernels: 122 us -> 91.1 us
    pallas_call x1, Pallas kernels: 122 us -> 91.1 us  [on_device(): pl.pallas_call(kernel, out_shape=[jax.ShapeDtypeStruct((4, 3, 1, NWIN), F...]
where the time goes in v3:
time: 96.9 us; the launch traced here: 96.6 us
  Pallas kernels  91.1 us (94%)
  local copies, waits for them, and re-layouts  3.49 us (4%)
  other arithmetic  1.36 us (1%)
    pallas_call x1, Pallas kernels, on_device(): pl.pallas_call(kernel, out_shape=[jax.ShapeDtypeStruct((4, 3, 1, NWIN), F...  91.1 us
    unnamed x3, local copies, waits for them, and re-layouts  3.22 us

profile of v3, /device:TPU:1, one launch (start us, length us, event | category | flops | bytes accessed | tf_op | source)
XLA Modules:
  0.0 96.6 jit_solution(7124838063451458760)
XLA Ops:
  0.6 0.7 bitcast_add_fusion
  1.3 0.1 reshape.16
  1.4 0.1 reshape.17
  1.5 0.7 copy.9
  2.2 0.1 reshape.15
  2.3 0.7 pad_add_fusion.meta
  3.0 91.1 %shard_map.59 = (f32[4,3,1,15]{3,2,1,0:T(1,128)}, f32[3,128]{1,0:T(4,128)}) custom-call(bf16[2,48,48,384]{3,2,1,0:T(8,128)(2,1)} %frames.1, s32[8,128]{1,0:T(8,128)} %pad_add_fusion.meta), custom_call_target="tpu_custom_call" | custom-call | tf_op jit(solution)/shard_map/pallas_call | solution.py:502
  94.1 1.3 %copy.12 = f32[4,3,1,15]{3,2,1,0:T(1,128)} copy(f32[4,3,1,15]{3,2,1,0:T(1,128)} %get-tuple-element.4) | data formatting | bytes 1440
  95.4 1.2 %copy.13 = f32[3,128]{1,0:T(4,128)} copy(f32[3,128]{1,0:T(4,128)} %get-tuple-element.5) | data formatting | bytes 3072
  (4 shorter events, 0.0 us)

commit v4 on v3

--- a/solution.py
+++ b/solution.py
@@ -20,8 +20,8 @@
 F32 = jnp.float32
 MESH = pl.DeviceIdType.MESH
 
-PASS_STEPS = {2: 6, 1: 10, 0: 15}
-SEND_STEPS = (1, 5, 9, 12)
+PASS_STEPS = {2: 6, 1: 10, 0: 14}
+SEND_STEPS = (2, 6, 10, 13)
 
 
 def lane(shape):
@@ -161,6 +161,22 @@
     greeted += [(twin, lax.rem(s + 1, NS)), (twin, lax.rem(s + NS - 1, NS))]
     for device in greeted:
         pl.semaphore_signal(barrier, inc=1, device_id=device, device_id_type=MESH)
+    @pl.when(s == 0)
+    def _():
+        for slot in range(5):
+            F[slot, 0:H] = jnp.zeros((H, W, 384), BF)
+
+    @pl.when(s == NS - 1)
+    def _():
+        for slot in range(5):
+            F[slot, H + W :] = jnp.zeros((H, W, 384), BF)
+
+    wide[:, :, :, :, 384:] = jnp.zeros((2, 2, EXT, W, 128), BF)
+    for right in (right0, right1):
+        right[48:96, 24 * 128 :] = jnp.zeros((W, 128), BF)
+        right[96:144, 0:128] = jnp.zeros((W, 128), BF)
+    sums[...] = jnp.zeros_like(sums)
+
     pl.semaphore_wait(barrier, len(greeted))
 
     def remote(src, dst, send, recv, device):
@@ -261,24 +277,8 @@
     for side in range(2):
         meta_copy(side).start()
 
-    @pl.when(s == 0)
-    def _():
-        for slot in range(5):
-            F[slot, 0:H] = jnp.zeros((H, W, 384), BF)
-
-    @pl.when(s == NS - 1)
-    def _():
-        for slot in range(5):
-            F[slot, H + W :] = jnp.zeros((H, W, 384), BF)
-
-    wide[:, :, :, :, 384:] = jnp.zeros((2, 2, EXT, W, 128), BF)
-    for right in (right0, right1):
-        right[48:96, 24 * 128 :] = jnp.zeros((W, 128), BF)
-        right[96:144, 0:128] = jnp.zeros((W, 128), BF)
-    sums[...] = jnp.zeros_like(sums)
-
-    end_halo(own[1], 0, 1, 2, tm)
-    for k in (1, 0):
+    def next_own(k):
+        end_halo(own[1], 0, 1, k + 1, tm)
         start_halo(own[1], 0, 1, k, tm)
 
     def key_copy(o):
@@ -322,20 +322,22 @@
 
             lax.fori_loop(0, NT, put, 0)
 
-    def stage(pair, k):
+    def stage(pair, k, core_layers=True, rim=True):
         first, second, side = firsts[3], seconds[3], lax.rem(pair, 2)
         for p in range(3):
             first = jnp.where(pair == p, firsts[p], first)
             second = jnp.where(pair == p, seconds[p], second)
         at = pl.ds(pl.multiple_of(128 * k, 128), 128)
-        for b in range(0, W, 8):
-            part = F[first, H + b : H + b + 8, :, at]
-            planes[side, 0, b : b + 8, :, at] = part
-            planes[side, 1, b : b + 8, :, at] = pltpu.roll(part, 64, 2)
+        if core_layers:
+            for b in range(0, W, 8):
+                part = F[first, H + b : H + b + 8, :, at]
+                planes[side, 0, b : b + 8, :, at] = part
+                planes[side, 1, b : b + 8, :, at] = pltpu.roll(part, 64, 2)
         for b in range(0, EXT, 8):
-            part = F[second, b : b + 8, :, at]
-            wide[side, 0, b : b + 8, :, at] = part
-            wide[side, 1, b : b + 8, :, at] = pltpu.roll(part, 64, 2)
+            if core_layers if H <= b < H + W else rim:
+                part = F[second, b : b + 8, :, at]
+                wide[side, 0, b : b + 8, :, at] = part
+                wide[side, 1, b : b + 8, :, at] = pltpu.roll(part, 64, 2)
 
     def pass_on(k):
         each_across((k,), outer, received)
@@ -345,10 +347,14 @@
             start_halo(F.at[slot], H, slot, k, tm, uses)
 
     def twin_halos():
-        for k in (1, 0):
-            end_halo(own[1], 0, 1, k, tm)
+        end_halo(own[1], 0, 1, 0, tm)
         for k in (2, 1, 0):
             start_halo(own[0], 0, 2, k, twin, core == 1)
+
+    def own_rim(k):
+        if k == 1:
+            next_own(0)
+        got_halo(1, k)
 
     def got_twin(k):
         if k == 2:
@@ -381,15 +387,22 @@
 
     for i in range(2):
         local(i).wait()
+    pltpu.make_async_copy(meta, scalars, ss).wait()
+
+    def own_core(k, _):
+        stage(0, k, rim=False)
+        return 0
+
+    lax.fori_loop(0, 3, own_core, 0)
+    next_own(1)
     got_halo(1, 2)
-    pltpu.make_async_copy(meta, scalars, ss).wait()
-    stage(0, 2)
+    stage(0, 2, core_layers=False)
     prepare(0, left0, right0)
     events = [
-        (1, functools.partial(got_halo, 1, 1)),
+        (1, functools.partial(own_rim, 1)),
         (2, share_keys),
         (3, twin_halos),
-        (4, functools.partial(got_halo, 1, 0)),
+        (4, functools.partial(own_rim, 0)),
         (5, mark_cells),
         (7, functools.partial(got_twin, 2)),
         (8, functools.partial(got_twin, 1)),
@@ -403,9 +416,13 @@
         for at, event in events:
             pl.when(h == at)(event)
 
-        @pl.when((h == 1) | (h == 4) | (h == 7) | (h == 8) | (h == 11))
+        @pl.when((h == 1) | (h == 4))
         def _():
-            stage(jnp.where(h < 7, 0, 1), jnp.where(h == 7, 2, jnp.where((h == 1) | (h == 8), 1, 0)))
+            stage(0, jnp.where(h == 1, 1, 0), core_layers=False)
+
+        @pl.when((h == 7) | (h == 8) | (h == 11))
+        def _():
+            stage(1, jnp.where(h == 7, 2, jnp.where(h == 8, 1, 0)))
 
         @pl.when((h == 14) | (h == 17) | (h == 23))
         def _():

time: 96.9 us -> 94.7 us (0.977)
  Pallas kernels: 91.1 us -> 89 us
    pallas_call x1, Pallas kernels: 91.1 us -> 89 us  [on_device(): pl.pallas_call(kernel, out_shape=[jax.ShapeDtypeStruct((4, 3, 1, NWIN), F...]
where the time goes in v4:
time: 94.7 us; the launch traced here: 94.5 us
  Pallas kernels  89 us (94%)
  local copies, waits for them, and re-layouts  3.49 us (4%)
  other arithmetic  1.36 us (1%)
    pallas_call x1, Pallas kernels, on_device(): pl.pallas_call(kernel, out_shape=[jax.ShapeDtypeStruct((4, 3, 1, NWIN), F...  89 us
    unnamed x3, local copies, waits for them, and re-layouts  3.22 us

profile of v4, /device:TPU:1, one launch (start us, length us, event | category | flops | bytes accessed | tf_op | source)
XLA Modules:
  0.0 94.5 jit_solution(9208649115669560433)
XLA Ops:
  0.6 0.7 bitcast_add_fusion
  1.3 0.1 reshape.16
  1.4 0.1 reshape.17
  1.5 0.7 copy.9
  2.2 0.1 reshape.15
  2.3 0.7 pad_add_fusion.meta
  3.0 89.0 %shard_map.59 = (f32[4,3,1,15]{3,2,1,0:T(1,128)}, f32[3,128]{1,0:T(4,128)}) custom-call(bf16[2,48,48,384]{3,2,1,0:T(8,128)(2,1)} %frames.1, s32[8,128]{1,0:T(8,128)} %pad_add_fusion.meta), custom_call_target="tpu_custom_call" | custom-call | tf_op jit(solution)/shard_map/pallas_call | solution.py:519
  92.0 1.3 %copy.12 = f32[4,3,1,15]{3,2,1,0:T(1,128)} copy(f32[4,3,1,15]{3,2,1,0:T(1,128)} %get-tuple-element.4) | data formatting | bytes 1440
  93.3 1.2 %copy.13 = f32[3,128]{1,0:T(4,128)} copy(f32[3,128]{1,0:T(4,128)} %get-tuple-element.5) | data formatting | bytes 3072
  (4 shorter events, 0.0 us)

commit v5 on v4

--- a/solution.py
+++ b/solution.py
@@ -8,6 +8,7 @@
 from jax.sharding import PartitionSpec as P
 
 W = 48
+STEP = 2
 H = 16
 S = 24
 NWIN = 15
@@ -15,72 +16,64 @@
 NS = 16
 NT = 8
 EXT = W + 2 * H
-DEPTH = 25 * 128
 BF = jnp.bfloat16
 F32 = jnp.float32
 MESH = pl.DeviceIdType.MESH
 
-PASS_STEPS = {2: 6, 1: 10, 0: 14}
-SEND_STEPS = (2, 6, 10, 13)
+PASS_STEPS = {2: 6, 1: 9, 0: 13}
+SEND_STEPS = (2, 7, 12, 14)
 
 
 def lane(shape):
     return lax.broadcasted_iota(jnp.int32, shape, len(shape) - 1)
 
 
-def prepare_first(planes, side, w, right):
+def correlate(planes, wide, side, w, qx, qy, qz, row, sums):
     start = S * w
     tile = start // 128
-    offset = start - 128 * tile
-    here = pl.ds(pl.multiple_of(128 * tile, 128), 128)
-    there = pl.ds(pl.multiple_of(128 * lax.min(tile + 1, 2), 128), 128)
-    c = lane((1, 1, 128))
-    d = jnp.where(c >= 64, c - 64, c + 64)
-    keep = [((v >= offset) & (v < offset + W), v + 128 < offset + W) for v in (c, d)]
-    zero = jnp.zeros((2, W, 128), BF)
-    previous = None
-    for j in range(24):
-        low, high = [
-            jnp.where(
-                keep[r][0],
-                planes[side, r, 2 * j : 2 * j + 2, :, here],
-                jnp.where(keep[r][1], planes[side, r, 2 * j : 2 * j + 2, :, there], zero),
-            )
-            for r in range(2)
-        ]
-        even = low[0] + high[1]
-        right[48:96, j * 128 : j * 128 + 128] = even
-        right[96:144, j * 128 + 128 : j * 128 + 256] = even
-        right[0:48, j * 128 : j * 128 + 128] = high[0] if previous is None else high[0] + previous
-        previous = low[1]
-    right[0:48, 24 * 128 :] = previous
-
-
-def prepare_second(wide, side, w, qx, qz, left):
-    start = S * w
-    base = start - 128 * (start // 128)
-    tile = (start + 112) // 128
-    offset = start + qz - 1 - 128 * (tile - 1)
-    here = pl.ds(pl.multiple_of(128 * lax.rem(tile + 3, 4), 128), 128)
-    there = pl.ds(pl.multiple_of(128 * tile, 128), 128)
+    base = start - 128 * tile
+    here = pl.ds(pl.multiple_of(128 * jnp.where(base > 128 - W, tile + 3, tile), 128), 128)
     c = lane((1, 128))
     d = jnp.where(c >= 64, c - 64, c + 64)
-    first, first_turned = c >= offset, d >= offset
+    low, high = [lax.rem(v + 128 - base, 128) < W for v in (c, d)]
+    zero = jnp.zeros((W, 128), BF)
+
+    def first_pair(x):
+        pair = zero if x + 1 == W else jnp.where(high, planes[side, 1, x + 1, :, here], zero)
+        return pair if x < 0 else jnp.where(low, planes[side, 0, x, :, here], pair)
+
+    second_tile = (start + 112) // 128
+    offset = start + qz - 1 - 128 * (second_tile - 1)
+    before = pl.ds(pl.multiple_of(128 * lax.rem(second_tile + 3, 4), 128), 128)
+    after = pl.ds(pl.multiple_of(128 * second_tile, 128), 128)
+    early, early_turned = c >= offset, d >= offset
     slot = lax.rem(c + 256 - offset, 128) < 64
-    turn = base - offset + 512
-    for j in range(25):
+    turns = [lax.rem(base - offset + 512 - e, 128) for e in range(3)]
+
+    def second_pair(j):
         x = H - 1 + qx + 2 * j
-        even = jnp.where(first, wide[side, 0, x, :, here], wide[side, 0, x, :, there])
-        odd = jnp.where(first_turned, wide[side, 1, x + 1, :, here], wide[side, 1, x + 1, :, there])
+        even = jnp.where(early, wide[side, 0, x, :, before], wide[side, 0, x, :, after])
+        odd = jnp.where(early_turned, wide[side, 1, x + 1, :, before], wide[side, 1, x + 1, :, after])
         pair = jnp.where(slot, even, odd)
-        for e in range(3):
-            left[48 * e : 48 * e + 48, j * 128 : j * 128 + 128] = pltpu.roll(
-                pair, lax.rem(turn - e, 128), 1
-            )
-
-
-def correlate(left, right, qy, row, sums):
-    c = lax.dot_general(left[...], right[...], (((1,), (1,)), ((), ())), preferred_element_type=F32)
+        return jnp.concatenate([pltpu.roll(pair, turn, 1) for turn in turns], axis=0)
+
+    products, last = None, zero
+    for j0 in range(0, 25, STEP):
+        left, right = [], []
+        for j in range(j0, min(j0 + STEP, 25)):
+            left.append(second_pair(j))
+            even = first_pair(2 * j) if 2 * j < W else zero
+            odd = first_pair(2 * j - 1)
+            right.append(jnp.concatenate([odd, even, last], axis=0))
+            last = even
+        part = lax.dot_general(
+            jnp.concatenate(left, axis=1),
+            jnp.concatenate(right, axis=1),
+            (((1,), (1,)), ((), ())),
+            preferred_element_type=F32,
+        )
+        products = part if products is None else products + part
+    c = products
     column = lax.broadcasted_iota(jnp.int32, (W, 144), 1)
     y = jnp.where(column < 48, column, jnp.where(column < 96, column - 48, column - 96))
     lag = lax.broadcasted_iota(jnp.int32, (W, 144), 0) - y - qy
@@ -137,7 +130,7 @@
 
 def kernel(
     frames, meta, velocity_out, tile_out,
-    F, wide, planes, left0, left1, right0, right1, sums, hot,
+    F, wide, planes, sums, hot,
     metas, mine, scalars, keys, vector, vectors, beside, parts, arrived,
     local_sem, xs, xr, cs, cr, hs, hr, ms, mr, ss, ks, kr, vs, vr, bs, br, ps, pr,
 ):
@@ -172,9 +165,6 @@
             F[slot, H + W :] = jnp.zeros((H, W, 384), BF)
 
     wide[:, :, :, :, 384:] = jnp.zeros((2, 2, EXT, W, 128), BF)
-    for right in (right0, right1):
-        right[48:96, 24 * 128 :] = jnp.zeros((W, 128), BF)
-        right[96:144, 0:128] = jnp.zeros((W, 128), BF)
     sums[...] = jnp.zeros_like(sums)
 
     pl.semaphore_wait(barrier, len(greeted))
@@ -327,12 +317,22 @@
         for p in range(3):
             first = jnp.where(pair == p, firsts[p], first)
             second = jnp.where(pair == p, seconds[p], second)
-        at = pl.ds(pl.multiple_of(128 * k, 128), 128)
+        at, across_at, next_at = [
+            pl.ds(pl.multiple_of(128 * t, 128), 128) for t in (k, 3 + lax.min(k, 1), lax.min(k + 1, 2))
+        ]
+        upper = lane((1, 1, 128)) >= 64
         if core_layers:
             for b in range(0, W, 8):
                 part = F[first, H + b : H + b + 8, :, at]
+                turned = pltpu.roll(part, 64, 2)
                 planes[side, 0, b : b + 8, :, at] = part
-                planes[side, 1, b : b + 8, :, at] = pltpu.roll(part, 64, 2)
+                planes[side, 1, b : b + 8, :, at] = turned
+                planes[side, 0, b : b + 8, :, across_at] = jnp.where(
+                    upper, part, planes[side, 0, b : b + 8, :, next_at]
+                )
+                planes[side, 1, b : b + 8, :, across_at] = jnp.where(
+                    upper, planes[side, 1, b : b + 8, :, next_at], turned
+                )
         for b in range(0, EXT, 8):
             if core_layers if H <= b < H + W else rim:
                 part = F[second, b : b + 8, :, at]
@@ -373,31 +373,23 @@
         w = jnp.where(i < 15, 14 - i, jnp.where(i < 30, 29 - i, 14 - (late + 30) // 2 + 15))
         return pair, w
 
-    def prepare(i, left, right):
+    def window(i):
         pair, w = item(i)
         at = 16 * pair + w
-        side = lax.rem(pair, 2)
-        prepare_first(planes, side, w, right)
-        prepare_second(wide, side, w, scalars[0, at], scalars[2, at], left)
-
-    def finish(i, left, right):
-        pair, w = item(i)
-        at = 16 * pair + w
-        correlate(left, right, scalars[1, at], at, sums)
+        correlate(planes, wide, lax.rem(pair, 2), w, scalars[0, at], scalars[1, at], scalars[2, at], at, sums)
 
     for i in range(2):
         local(i).wait()
     pltpu.make_async_copy(meta, scalars, ss).wait()
 
     def own_core(k, _):
-        stage(0, k, rim=False)
+        stage(0, 2 - k, rim=False)
         return 0
 
     lax.fori_loop(0, 3, own_core, 0)
     next_own(1)
     got_halo(1, 2)
     stage(0, 2, core_layers=False)
-    prepare(0, left0, right0)
     events = [
         (1, functools.partial(own_rim, 1)),
         (2, share_keys),
@@ -405,12 +397,12 @@
         (4, functools.partial(own_rim, 0)),
         (5, mark_cells),
         (7, functools.partial(got_twin, 2)),
-        (8, functools.partial(got_twin, 1)),
-        (11, functools.partial(got_twin, 0)),
+        (9, functools.partial(got_twin, 1)),
+        (12, functools.partial(got_twin, 0)),
     ]
     events += [(at, functools.partial(next_across, *send)) for at, send in zip(SEND_STEPS, sends)]
     events += [(at, functools.partial(pass_on, k)) for k, at in PASS_STEPS.items()]
-    events += [(at, functools.partial(got_across, k)) for k, at in ((2, 14), (1, 17), (0, 23))]
+    events += [(at, functools.partial(got_across, k)) for k, at in ((2, 15), (1, 18), (0, 24))]
 
     def step(h, _):
         for at, event in events:
@@ -420,22 +412,20 @@
         def _():
             stage(0, jnp.where(h == 1, 1, 0), core_layers=False)
 
-        @pl.when((h == 7) | (h == 8) | (h == 11))
+        @pl.when((h == 7) | (h == 9) | (h == 12))
         def _():
-            stage(1, jnp.where(h == 7, 2, jnp.where(h == 8, 1, 0)))
-
-        @pl.when((h == 14) | (h == 17) | (h == 23))
+            stage(1, jnp.where(h == 7, 2, jnp.where(h == 9, 1, 0)))
+
+        @pl.when((h == 15) | (h == 18) | (h == 24))
         def _():
             def both(pair, _):
-                stage(pair, jnp.where(h == 14, 2, jnp.where(h == 17, 1, 0)))
+                stage(pair, jnp.where(h == 15, 2, jnp.where(h == 18, 1, 0)))
                 return 0
 
             lax.fori_loop(2, 4, both, 0)
 
-        prepare(2 * h + 1, left1, right1)
-        finish(2 * h, left0, right0)
-        prepare(lax.min(2 * h + 2, 59), left0, right0)
-        finish(2 * h + 1, left1, right1)
+        window(2 * h)
+        window(2 * h + 1)
         return 0
 
     lax.fori_loop(0, 30, step, 0)
@@ -524,11 +514,7 @@
         scratch_shapes=[
             vmem((5, EXT, W, 384), BF),
             vmem((2, 2, EXT, W, 512), BF),
-            vmem((2, 2, W, W, 384), BF),
-            vmem((144, DEPTH), BF),
-            vmem((144, DEPTH), BF),
-            vmem((144, DEPTH), BF),
-            vmem((144, DEPTH), BF),
+            vmem((2, 2, W, W, 640), BF),
             vmem((6, 64, 128), F32),
             vmem((NT * CELLS, NS * 64), BF),
             vmem((2, 8, 128), jnp.int32),

time: 94.7 us -> 87.6 us (0.925)
  Pallas kernels: 89 us -> 81.8 us
    pallas_call x1, Pallas kernels: 89 us -> 81.8 us  [on_device(): pl.pallas_call(kernel, out_shape=[jax.ShapeDtypeStruct((4, 3, 1, NWIN), F...]
where the time goes in v5:
time: 87.6 us; the launch traced here: 87.3 us
  Pallas kernels  81.8 us (93%)
  local copies, waits for them, and re-layouts  3.49 us (4%)
  other arithmetic  1.36 us (2%)
    pallas_call x1, Pallas kernels, on_device(): pl.pallas_call(kernel, out_shape=[jax.ShapeDtypeStruct((4, 3, 1, NWIN), F...  81.8 us
    unnamed x3, local copies, waits for them, and re-layouts  3.22 us

profile of v5, /device:TPU:1, one launch (start us, length us, event | category | flops | bytes accessed | tf_op | source)
XLA Modules:
  0.0 87.3 jit_solution(5391217288965046492)
XLA Ops:
  0.6 0.7 bitcast_add_fusion
  1.3 0.1 reshape.16
  1.4 0.1 reshape.17
  1.5 0.7 copy.9
  2.2 0.1 reshape.15
  2.3 0.7 pad_add_fusion.meta
  3.0 81.8 %shard_map.59 = (f32[4,3,1,15]{3,2,1,0:T(1,128)}, f32[3,128]{1,0:T(4,128)}) custom-call(bf16[2,48,48,384]{3,2,1,0:T(8,128)(2,1)} %frames.1, s32[8,128]{1,0:T(8,128)} %pad_add_fusion.meta), custom_call_target="tpu_custom_call" | custom-call | tf_op jit(solution)/shard_map/pallas_call | solution.py:509
  84.8 1.3 %copy.12 = f32[4,3,1,15]{3,2,1,0:T(1,128)} copy(f32[4,3,1,15]{3,2,1,0:T(1,128)} %get-tuple-element.4) | data formatting | bytes 1440
  86.1 1.2 %copy.13 = f32[3,128]{1,0:T(4,128)} copy(f32[3,128]{1,0:T(4,128)} %get-tuple-element.5) | data formatting | bytes 3072
  (4 shorter events, 0.0 us)

commit v6 on v5

--- a/solution.py
+++ b/solution.py
@@ -20,8 +20,8 @@
 F32 = jnp.float32
 MESH = pl.DeviceIdType.MESH
 
-PASS_STEPS = {2: 6, 1: 9, 0: 13}
-SEND_STEPS = (2, 7, 12, 14)
+PASS_STEPS = {2: 6, 1: 9, 0: 14}
+SEND_STEPS = (2, 7, 14)
 
 
 def lane(shape):
@@ -204,15 +204,16 @@
 
     outer, inner = (0, 1), (2,)
 
-    def next_across(past, past_parts, ks, parts):
-        each_across(past, past_parts, sent)
-        each_across(ks, parts, begin)
+    def next_across(past, following):
+        for group in past:
+            each_across(*group, sent)
+        for group in following:
+            each_across(*group, begin)
 
     sends = (
-        ((2,), outer, (1,), outer),
-        ((1,), outer, (0,), outer),
-        ((0,), outer, (2,), inner),
-        ((2,), inner, (1, 0), inner),
+        ([((2,), outer)], [((1,), outer)]),
+        ([((1,), outer)], [((0,), outer), ((2,), inner)]),
+        ([((0,), outer), ((2,), inner)], [((1, 0), inner)]),
     )
 
     def over():

time: 87.6 us -> 86.2 us (0.984)
  Pallas kernels: 81.8 us -> 80.4 us
    pallas_call x1, Pallas kernels: 81.8 us -> 80.4 us  [on_device(): pl.pallas_call(kernel, out_shape=[jax.ShapeDtypeStruct((4, 3, 1, NWIN), F...]
where the time goes in v6:
time: 86.2 us; the launch traced here: 85.9 us
  Pallas kernels  80.4 us (93%)
  local copies, waits for them, and re-layouts  3.49 us (4%)
  other arithmetic  1.36 us (2%)
    pallas_call x1, Pallas kernels, on_device(): pl.pallas_call(kernel, out_shape=[jax.ShapeDtypeStruct((4, 3, 1, NWIN), F...  80.4 us
    unnamed x3, local copies, waits for them, and re-layouts  3.22 us

profile of v6, /device:TPU:1, one launch (start us, length us, event | category | flops | bytes accessed | tf_op | source)
XLA Modules:
  0.0 85.9 jit_solution(12406982294767401580)
XLA Ops:
  0.6 0.7 bitcast_add_fusion
  1.3 0.1 reshape.16
  1.4 0.1 reshape.17
  1.5 0.7 copy.9
  2.2 0.1 reshape.15
  2.3 0.7 pad_add_fusion.meta
  3.0 80.4 %shard_map.59 = (f32[4,3,1,15]{3,2,1,0:T(1,128)}, f32[3,128]{1,0:T(4,128)}) custom-call(bf16[2,48,48,384]{3,2,1,0:T(8,128)(2,1)} %frames.1, s32[8,128]{1,0:T(8,128)} %pad_add_fusion.meta), custom_call_target="tpu_custom_call" | custom-call | tf_op jit(solution)/shard_map/pallas_call | solution.py:510
  83.4 1.3 %copy.12 = f32[4,3,1,15]{3,2,1,0:T(1,128)} copy(f32[4,3,1,15]{3,2,1,0:T(1,128)} %get-tuple-element.4) | data formatting | bytes 1440
  84.7 1.2 %copy.13 = f32[3,128]{1,0:T(4,128)} copy(f32[3,128]{1,0:T(4,128)} %get-tuple-element.5) | data formatting | bytes 3072
  (4 shorter events, 0.0 us)
